TPU v7x, 256 devices: a whole 4x4x8 slice. The times are simulated.
256 devices in a mesh: seq: 4 (over x), head: 64 (over z, y, core).
Axes of the slice: x: 4, y: 4, z: 8, core: 2. Of those that a mesh axis runs over, the one named last changes fastest.
Arguments:
- queries: bfloat16 [2048, 40960], P(('seq', 'head'))
- keys: bfloat16 [2048, 40960], P(('seq', 'head'))
- values: bfloat16 [2048, 40960], P(('seq', 'head')), may hold values from -6 to 6
- block_mask: int32 [64, 16, 9], P('head'), may hold values 0 or 1
- prompt_lengths: int32 [4], replicated, may hold values from 1 to 1024, 2048 in all
Outputs:
- attended: bfloat16 [2048, 40960], P(('seq', 'head'))
Inputs may be any that keep to these rules, and one draw needn't show every extreme that they name: `prompt_lengths`: the lengths sum to 2048; the longest prompt has exactly 1024 tokens.
All inputs are finite; a program needn't handle non-finite values. No bound on the sum of `block_mask` on one device may be relied on, other than what follows from the above.
Results may differ from a plain program's by a relative error of at most 0.009.
Values may be sent and summed in bfloat16 or wider, within the bound.
No kernel may reach another device: no remote copies, remote signals or barrier semaphores. Data moves between devices by JAX's collectives and lax.ppermute only.
A program may use at most 64 MiB of HBM per device.

v0:
```python
import jax
import jax.numpy as jnp
from jax import lax
from jax.sharding import PartitionSpec as P

HEAD_DIM = 128
BLOCK = 128


neg_big = -1e30


def padded(block, sides, width):
    for axis, dim in sides:
        count = lax.axis_size(axis)
        forward = [(i, i + 1) for i in range(count - 1)]
        backward = [(target, source) for source, target in forward]
        low = lax.ppermute(
            lax.slice_in_dim(block, block.shape[dim] - width, None, axis=dim), axis, forward
        )
        high = lax.ppermute(lax.slice_in_dim(block, 0, width, axis=dim), axis, backward)
        block = jnp.concatenate([low, block, high], axis=dim)
    return block


def segment_of(positions, ends):
    return jnp.sum((positions[:, None] >= ends[None, :]).astype(jnp.int32), axis=1)


def attend(q_rows, k_rows, v_rows, q_start, k_start, mask_table, ends, reach, tokens_all):
    count_q = q_rows.shape[0]
    count_k = k_rows.shape[0]
    heads = q_rows.shape[1] // HEAD_DIM
    span = 2 * reach + 1
    scale = 1.0 / HEAD_DIM**0.5
    q_pos = q_start + jnp.arange(count_q, dtype=jnp.int32)
    k_pos = k_start + jnp.arange(count_k, dtype=jnp.int32)
    valid = (k_pos >= 0) & (k_pos < tokens_all)
    same_seg = segment_of(q_pos, ends)[:, None] == segment_of(k_pos, ends)[None, :]
    q_first = q_start // BLOCK
    mask_rows = lax.dynamic_slice_in_dim(mask_table, q_first + reach, count_q // BLOCK, 0)
    q_blocks = q_first + jnp.arange(count_q // BLOCK, dtype=jnp.int32)
    k_blocks = k_start // BLOCK + jnp.arange(count_k // BLOCK, dtype=jnp.int32)
    offset = k_blocks[None, :] - q_blocks[:, None] + reach
    lookup = (offset[:, None, :] == jnp.arange(span, dtype=jnp.int32)[None, :, None]).astype(
        jnp.int32
    )
    hits = jnp.sum(mask_rows[:, :, None] * lookup, axis=1)
    block_ok = (hits > 0) | (offset == reach)
    token_ok = jnp.repeat(jnp.repeat(block_ok, BLOCK, axis=0), BLOCK, axis=1)
    allowed = token_ok & same_seg & valid[None, :]
    maxima, totals, outputs = ([], [], [])
    for head in range(heads):
        lo = head * HEAD_DIM
        q_head = q_rows[:, lo : lo + HEAD_DIM]
        k_head = k_rows[:, lo : lo + HEAD_DIM]
        v_head = v_rows[:, lo : lo + HEAD_DIM]
        scores = jnp.einsum("qd,kd->qk", q_head, k_head, preferred_element_type=jnp.float32) * scale
        scores = jnp.where(allowed, scores, neg_big)
        row_max = jnp.max(scores, axis=1)
        weights = jnp.where(allowed, jnp.exp(scores - row_max[:, None]), 0.0)
        maxima.append(row_max)
        totals.append(jnp.sum(weights, axis=1))
        outputs.append(
            jnp.dot(weights.astype(jnp.bfloat16), v_head, preferred_element_type=jnp.float32)
        )
    return (jnp.stack(maxima), jnp.stack(totals), jnp.stack(outputs))


def finish(run_total, run_out):
    mixed = (run_out / run_total[:, :, None]).astype(jnp.bfloat16)
    return jnp.transpose(mixed, (1, 0, 2)).reshape(mixed.shape[1], mixed.shape[0] * mixed.shape[2])


def body(queries, keys, values, block_mask, prompt_lengths):
    q_local, k_local, v_local = (
        lax.all_to_all(queries, "head", split_axis=1, concat_axis=0, tiled=True),
        lax.all_to_all(keys, "head", split_axis=1, concat_axis=0, tiled=True),
        lax.all_to_all(values, "head", split_axis=1, concat_axis=0, tiled=True),
    )
    rows = q_local.shape[0]
    reach = (block_mask.shape[2] - 1) // 2
    tokens_all = block_mask.shape[1] * BLOCK
    ends = jnp.cumsum(prompt_lengths)[:-1]
    first = lax.axis_index("seq") * rows
    mask_table = jnp.pad(block_mask[0], ((reach, reach), (0, 0)))
    stacked = jnp.stack((k_local, v_local))
    extended = padded(stacked, (("seq", 1),), rows)
    k_ext = extended[0]
    v_ext = extended[1]
    run_max, run_total, run_out = attend(
        q_local, k_ext, v_ext, first, first - rows, mask_table, ends, reach, tokens_all
    )
    mixed = finish(run_total, run_out)
    return lax.all_to_all(mixed, "head", split_axis=0, concat_axis=1, tiled=True)


def solution(mesh):
    placed = (
        P(("seq", "head"), None),
        P(("seq", "head"), None),
        P(("seq", "head"), None),
        P("head", None, None),
        P(),
    )
    return jax.shard_map(
        body, mesh=mesh, in_specs=placed, out_specs=P(("seq", "head"), None), check_vma=False
    )
```

profile of v0, /device:TPU:1, one launch (start us, length us, event | category | flops | bytes accessed | tf_op | source)
XLA Modules:
  0.0 158.9 jit_solution(3933958076183204568)
XLA Ops:
  0.0 33.5 %all_to_all.70 = bf16[8,64,640]{2,0,1:T(8,128)(2,1)S(1)} all-to-all(bf16[8,64,640]{2,0,1:T(8,128)(2,1)} %bitcast.102), channel_id=1, replica_groups=mesh['seq'=4,'head'=64] {'head'}, dimensions={1} | all-to-all | bytes 1310720 | tf_op jit(solution)/shard_map/all_to_all | solution.py:78
  33.5 5.9 %all-to-all-start.1 = ((bf16[8,64,640]{2,0,1:T(8,128)(2,1)}), bf16[8,64,640]{2,0,1:T(8,128)(2,1)S(1)}, u32[]{:S(2)}, u32[]{:S(2)}) async-start(bf16[8,64,640]{2,0,1:T(8,128)(2,1)} %bitcast.103), calls=%async_computation.1 | async-start | bytes 1310720 | tf_op jit(solution)/shard_map/all_to_all | solution.py:79
  39.4 0.8 reduce-window.4
  40.2 0.7 copy.16
  40.9 0.1 pad_dynamic-slice_fusion
  41.0 0.1 subtract_add_fusion
  41.1 18.6 %all-to-all-done.1 = bf16[8,64,640]{2,0,1:T(8,128)(2,1)S(1)} async-done(((bf16[8,64,640]{2,0,1:T(8,128)(2,1)}), bf16[8,64,640]{2,0,1:T(8,128)(2,1)S(1)}, u32[]{:S(2)}, u32[]{:S(2)}) %all-to-all-start.1) | async-done | bytes 655392 | tf_op jit(solution)/shard_map/all_to_all | solution.py:79
  59.7 5.9 %all-to-all-start.2 = ((bf16[8,64,640]{2,0,1:T(8,128)(2,1)}), bf16[8,64,640]{2,0,1:T(8,128)(2,1)S(1)}, u32[]{:S(2)}, u32[]{:S(2)}) async-start(bf16[8,64,640]{2,0,1:T(8,128)(2,1)} %bitcast.104), calls=%async_computation.2 | async-start | bytes 1310720 | tf_op jit(solution)/shard_map/all_to_all | solution.py:77
  65.6 1.2 pad_maximum_fusion.1
  66.8 1.3 collective-permute-start.1
  68.1 5.1 %collective-permute-start = (bf16[2,512,640]{2,1,0:T(8,128)(2,1)}, bf16[2,512,640]{2,1,0:T(8,128)(2,1)}, u32[]{:S(2)}, u32[]{:S(2)}) collective-permute-start(bf16[2,512,640]{2,1,0:T(8,128)(2,1)} %pad_maximum_fusion.1), channel_id=1, source_target_pairs={{0,64},{64,128},{128,192},{1,65},{65,129},{129,193},{2,66},{66,130... | collective-permute-start | bytes 3932168 | tf_op jit(solution)/shard_map/ppermute | solution.py:18
  73.2 0.1 select_reduce_fusion
  73.3 0.1 compare_or_fusion
  73.3 0.1 copy.11
  73.5 0.1 broadcast_bitcast_fusion
  73.6 0.1 convert_reduce_fusion.1
  73.7 0.1 convert_reduce_fusion
  73.8 1.3 fusion.10
  75.1 23.8 %collective-permute-done.1 = bf16[2,512,640]{2,1,0:T(8,128)(2,1)} collective-permute-done((bf16[2,512,640]{2,1,0:T(8,128)(2,1)}, bf16[2,512,640]{2,1,0:T(8,128)(2,1)}, u32[]{:S(2)}, u32[]{:S(2)}) %collective-permute-start.1) | collective-permute-done | bytes 1310752 | tf_op jit(solution)/shard_map/ppermute | solution.py:21
  98.9 0.9 collective-permute-done
  99.8 5.5 %pad_maximum_fusion = bf16[2,1536,640]{2,1,0:T(8,128)(2,1)S(1)} fusion(bf16[2,512,640]{2,1,0:T(8,128)(2,1)} %collective-permute-done.1, bf16[1,512,640]{2,1,0:T(8,128)(2,1)S(1)} %bitcast.95, bf16[1,512,640]{2,1,0:T(8,128)(2,1)S(1)} %bitcast.93, bf16[2,512,640]{2,1,0:T(8,128)(2,1)} %collective-permute-done), kind=kLoop, calls=%fused_computation | loop fusion | flops 15728640 | bytes 7864320 | tf_op jit(solution)/shard_map/concatenate | solution.py:22
  105.3 1.6 %slice_bitcast_fusion = (bf16[1536,640]{1,0:T(8,128)(2,1)S(1)}, bf16[1536,640]{1,0:T(8,128)(2,1)}) fusion(bf16[2,1536,640]{2,1,0:T(8,128)(2,1)S(1)} %pad_maximum_fusion), kind=kLoop, calls=%fused_computation.33 | loop fusion | bytes 7864320 | tf_op jit(solution)/shard_map/squeeze | solution.py:90
  106.9 0.0 all-to-all-done.2
  106.9 0.0 copy-start
  106.9 1.8 %fusion.96 = (f32[512]{0:T(512)S(1)}, f32[512,1536]{0,1:T(8,128)S(1)}) fusion(pred[512,1536]{0,1:T(32,128)(4,1)S(1)} %fusion.10, bf16[512,640]{1,0:T(8,128)(2,1)S(1)} %bitcast.96, bf16[1536,640]{1,0:T(8,128)(2,1)} %get-tuple-element.11), kind=kOutput, calls=%fused_computation.102 | convolution fusion | flops 203685376 | bytes 4458496 | tf_op jit(solution)/shard_map/qd,kd->qk/dot_general | solution.py:58
  108.7 0.0 copy-done
  108.7 0.7 fusion.95
  109.4 0.7 fusion.94
  110.1 0.7 fusion.93
  110.8 0.7 fusion.92
  111.5 1.6 fusion.44
  113.0 1.6 fusion.50
  114.6 1.6 fusion.56
  116.2 1.6 fusion.62
  117.7 4.0 %fusion.19 = (f32[512]{0:T(512)S(1)}, f32[512]{0:T(512)S(1)}, f32[512]{0:T(512)S(1)}, f32[512]{0:T(512)S(1)}, f32[512]{0:T(512)S(1)}) fusion(f32[512,1536]{0,1:T(8,128)S(1)} %get-tuple-element.21, f32[512]{0:T(512)S(1)} %get-tuple-element.20, pred[1536]{0:T(1024)(128)(4,1)S(1)} %compare_and_fusion, s32[1536]{0:T(1024)S(1)} %convert_reduce_fusion, ...), kind=kLoop, calls=%fused_computation.31 | loop fusion | flops 14153216 | bytes 15764992 | tf_op jit(solution)/shard_map/reduce_sum | solution.py:63
  121.8 1.6 fusion.68
  123.4 1.7 %fusion.71 = bf16[512,5,128]{2,0,1:T(8,128)(2,1)S(1)} fusion(f32[5,512,128]{2,1,0:T(8,128)} %fusion.68, f32[5,512]{1,0:T(8,128)S(1)} %stack.59), kind=kLoop, calls=%fused_computation.62 | loop fusion | flops 655360 | bytes 1976320 | tf_op jit(solution)/shard_map/transpose | solution.py:72
  125.1 0.5 copy.12
  125.6 0.8 all_to_all.62
  126.4 31.7 %all_to_all.71 = bf16[64,8,640]{2,1,0:T(8,128)(2,1)S(1)} all-to-all(bf16[64,8,640]{2,1,0:T(8,128)(2,1)S(1)} %all_to_all.62), channel_id=1, replica_groups=mesh['seq'=4,'head'=64] {'head'}, dimensions={0} | all-to-all | bytes 1310720 | tf_op jit(solution)/shard_map/all_to_all | solution.py:95
  158.1 0.8 copy.33
  (9 shorter events, 0.1 us)
Async XLA Ops:
  33.5 26.2 %all-to-all-start.1 = ((bf16[8,64,640]{2,0,1:T(8,128)(2,1)}), bf16[8,64,640]{2,0,1:T(8,128)(2,1)S(1)}, u32[]{:S(2)}, u32[]{:S(2)}) async-start(bf16[8,64,640]{2,0,1:T(8,128)(2,1)} %bitcast.103), calls=%async_computation.1 | async-start | bytes 1310720 | tf_op jit(solution)/shard_map/all_to_all | solution.py:79
  59.7 47.1 %all-to-all-start.2 = ((bf16[8,64,640]{2,0,1:T(8,128)(2,1)}), bf16[8,64,640]{2,0,1:T(8,128)(2,1)S(1)}, u32[]{:S(2)}, u32[]{:S(2)}) async-start(bf16[8,64,640]{2,0,1:T(8,128)(2,1)} %bitcast.104), calls=%async_computation.2 | async-start | bytes 1310720 | tf_op jit(solution)/shard_map/all_to_all | solution.py:77
  66.8 32.1 %collective-permute-start.1 = (bf16[2,512,640]{2,1,0:T(8,128)(2,1)}, bf16[2,512,640]{2,1,0:T(8,128)(2,1)}, u32[]{:S(2)}, u32[]{:S(2)}) collective-permute-start(bf16[2,512,640]{2,1,0:T(8,128)(2,1)} %pad_maximum_fusion.1), channel_id=1, source_target_pairs={{64,0},{128,64},{192,128},{65,1},{129,65},{193,129},{66,2},{130,66... | collective-permute-start | bytes 3932168 | tf_op jit(solution)/shard_map/ppermute | solution.py:21
  68.1 31.7 %collective-permute-start = (bf16[2,512,640]{2,1,0:T(8,128)(2,1)}, bf16[2,512,640]{2,1,0:T(8,128)(2,1)}, u32[]{:S(2)}, u32[]{:S(2)}) collective-permute-start(bf16[2,512,640]{2,1,0:T(8,128)(2,1)} %pad_maximum_fusion.1), channel_id=1, source_target_pairs={{0,64},{64,128},{128,192},{1,65},{65,129},{129,193},{2,66},{66,130... | collective-permute-start | bytes 3932168 | tf_op jit(solution)/shard_map/ppermute | solution.py:18
  106.9 1.8 %copy-start = (bf16[1536,640]{1,0:T(8,128)(2,1)S(1)}, bf16[1536,640]{1,0:T(8,128)(2,1)}, u32[]{:S(2)}) copy-start(bf16[1536,640]{1,0:T(8,128)(2,1)} %get-tuple-element.11) | copy-start | bytes 5898244
where the time goes:
time: 161 us; the launch traced here: 159 us
  blocking collectives  65.2 us (40%)
  waiting for transfers between devices  43.3 us (27%)
  starting transfers between devices  18.1 us (11%)
  other arithmetic  14.9 us (9%)
  matrix products  12.4 us (8%)
  local copies, waits for them, and re-layouts  4.72 us (3%)
    all_to_all x1, blocking collectives, body(): lax.all_to_all(keys, 'head', split_axis=1, concat_axis=0, tiled=True)  33.5 us
    all_to_all x1, blocking collectives, body(): lax.all_to_all(mixed, 'head', split_axis=0, concat_axis=1, tiled=True)  31.7 us
    ppermute x1, waiting for transfers between devices, padded(): lax.ppermute(lax.slice_in_dim(block, 0, width, axis=dim), axis, backward)  23.8 us
    all_to_all x1, waiting for transfers between devices, body(): lax.all_to_all(values, 'head', split_axis=1, concat_axis=0, tiled=True)  18.6 us
    dot_general x5, matrix products, attend(): jnp.dot(weights.astype(jnp.bfloat16), v_head, preferred_element_type=jnp....  7.84 us
    all_to_all x1, starting transfers between devices, body(): lax.all_to_all(queries, 'head', split_axis=1, concat_axis=0, tiled=True)  5.86 us
    all_to_all x1, starting transfers between devices, body(): lax.all_to_all(values, 'head', split_axis=1, concat_axis=0, tiled=True)  5.86 us
    concatenate x1, other arithmetic, padded(): block = jnp.concatenate([low, block, high], axis=dim)  5.48 us
  transfers between devices with their start and end apart: 4, of which 3 were waited for; matrix products, arithmetic and copies ran while one was open for 7% of the time, Pallas kernels for 0%

commit v1 on v0

v1 whole, which is shorter than its diff:
```python
import functools

import jax
import jax.numpy as jnp
from jax import lax
from jax.experimental import pallas as pl
from jax.experimental.pallas import tpu as pltpu
from jax.sharding import PartitionSpec as P

HEAD_DIM = 128
BLOCK = 128
neg_big = -1e30


def segment_of(positions, ends):
    seg = jnp.zeros_like(positions)
    for end in ends:
        seg = seg + (positions >= end).astype(jnp.int32)
    return seg


def attend_kernel(reach, tokens_all, lengths, first_ref, mask_ref, q_ref, kv_ref, left_ref, right_ref, out_ref):
    rows, cols = q_ref.shape
    heads = cols // HEAD_DIM
    blocks = rows // BLOCK
    span = 2 * reach + 1
    scale = 1.0 / HEAD_DIM**0.5
    first = first_ref[0]
    ends = []
    total = lengths[0]
    for i in range(1, lengths.shape[0]):
        ends.append(total)
        total = total + lengths[i]
    for b in range(blocks):
        q_pos = first + b * BLOCK + lax.broadcasted_iota(jnp.int32, (BLOCK, 1), 0)
        q_seg = segment_of(q_pos, ends)
        q_block = first // BLOCK + b
        bias = []
        for r in range(span):
            k_pos = first + (b + r - reach) * BLOCK + lax.broadcasted_iota(jnp.int32, (1, BLOCK), 1)
            k_seg = segment_of(k_pos, ends)
            k_block = q_block + r - reach
            ok = (k_block >= 0) & (k_block < tokens_all // BLOCK)
            if r != reach:
                ok = ok & (mask_ref[0, q_block, r] == 1)
            k_seg = jnp.where(ok, k_seg, -1)
            bias.append(jnp.where(q_seg == k_seg, 0.0, neg_big))
        bias = jnp.concatenate(bias, axis=1)
        here = slice(b * BLOCK, (b + 1) * BLOCK)
        parts = ((left_ref, slice(b * BLOCK, rows)), (kv_ref, slice(0, rows)), (right_ref, slice(0, (b + 1) * BLOCK)))
        for h in range(heads):
            k_cols = slice(h * HEAD_DIM, (h + 1) * HEAD_DIM)
            v_cols = slice(cols + h * HEAD_DIM, cols + (h + 1) * HEAD_DIM)
            q = q_ref[here, k_cols]
            scores = jnp.concatenate(
                [
                    lax.dot_general(
                        q, ref[part, k_cols], (((1,), (1,)), ((), ())), preferred_element_type=jnp.float32
                    )
                    for ref, part in parts
                ],
                axis=1,
            )
            scores = scores * scale + bias
            row_max = jnp.max(scores, axis=1, keepdims=True)
            weights = jnp.exp(scores - row_max)
            sums = jnp.sum(weights, axis=1, keepdims=True)
            weights = weights.astype(jnp.bfloat16)
            mixed = jnp.zeros((BLOCK, HEAD_DIM), jnp.float32)
            at = 0
            for ref, part in parts:
                width = part.stop - part.start
                mixed = mixed + jnp.dot(
                    weights[:, at : at + width], ref[part, v_cols], preferred_element_type=jnp.float32
                )
                at += width
            out_ref[here, k_cols] = (mixed / sums).astype(jnp.bfloat16)


def attend(prompt_lengths, first, block_mask, q, kv, left, right):
    reach = (block_mask.shape[2] - 1) // 2
    tokens_all = block_mask.shape[1] * BLOCK
    smem = pl.BlockSpec(memory_space=pltpu.SMEM)
    vmem = pl.BlockSpec(memory_space=pltpu.VMEM)
    return pl.pallas_call(
        functools.partial(attend_kernel, reach, tokens_all),
        out_shape=jax.ShapeDtypeStruct(q.shape, q.dtype),
        in_specs=[smem, smem, smem, vmem, vmem, vmem, vmem],
        out_specs=vmem,
        compiler_params=pltpu.CompilerParams(vmem_limit_bytes=40 * 1024 * 1024),
        cost_estimate=pl.CostEstimate(flops=1500000000, bytes_accessed=6000000, transcendentals=3000000),
    )(prompt_lengths, first, block_mask, q, kv, left, right)


def body(queries, keys, values, block_mask, prompt_lengths):
    groups = lax.axis_size("head")
    tokens, cols = queries.shape
    width = cols // groups
    both = jnp.concatenate(
        [keys.reshape(tokens, groups, width), values.reshape(tokens, groups, width)], axis=2
    ).reshape(tokens, 2 * cols)
    kv = lax.all_to_all(both, "head", split_axis=1, concat_axis=0, tiled=True)
    count = lax.axis_size("seq")
    left = lax.ppermute(kv, "seq", [(i, (i + 1) % count) for i in range(count)])
    right = lax.ppermute(kv, "seq", [((i + 1) % count, i) for i in range(count)])
    q = lax.all_to_all(queries, "head", split_axis=1, concat_axis=0, tiled=True)
    first = (lax.axis_index("seq") * q.shape[0]).astype(jnp.int32).reshape(1)
    mixed = attend(prompt_lengths, first, block_mask, q, kv, left, right)
    return lax.all_to_all(mixed, "head", split_axis=0, concat_axis=1, tiled=True)


def solution(mesh):
    placed = (
        P(("seq", "head"), None),
        P(("seq", "head"), None),
        P(("seq", "head"), None),
        P("head", None, None),
        P(),
    )
    return jax.shard_map(
        body, mesh=mesh, in_specs=placed, out_specs=P(("seq", "head"), None), check_vma=False
    )
```

time: 161 us -> 119 us (0.74); the launches traced: 159 us -> 119 us
  waiting for transfers between devices: 43.3 us -> 23.2 us
  other arithmetic: 14.9 us -> 1.38 us
  matrix products: 12.4 us -> 0 us
  Pallas kernels: 0 us -> 9.58 us
  blocking collectives: 65.2 us -> 74.7 us
  starting transfers between devices: 18.1 us -> 9.09 us
  local copies, waits for them, and re-layouts: 4.72 us -> 0.93 us
    ppermute x2, waiting for transfers between devices: 24.7 us -> 2.97 us  [the longest x1 2.96 us: body(): left = lax.ppermute(kv, 'seq', [(i, (i + 1) % count) for i in range(count)])]
    all_to_all x1, blocking collectives: 33.5 us -> 46.6 us  [body(): kv = lax.all_to_all(both, 'head', split_axis=1, concat_axis=0, tiled=True)]
    dot_general x10 -> x0, matrix products: 12.4 us -> none  [the longest x5 7.84 us: attend(): jnp.dot(weights.astype(jnp.bfloat16), v_head, preferred_element_type=jnp....]
    pallas_call x0 -> x1, Pallas kernels: none -> 9.58 us  [attend(): pl.pallas_call(functools.partial(attend_kernel, reach, tokens_all), out_s...]
    all_to_all x2 -> x1, starting transfers between devices: 11.7 us -> 6.61 us  [body(): q = lax.all_to_all(queries, 'head', split_axis=1, concat_axis=0, tiled=True)]
    reduce_sum x4 -> x0, other arithmetic: 4.26 us -> none  [the longest x1 4 us: attend(): totals.append(jnp.sum(weights, axis=1))]
    concatenate x1, other arithmetic: 5.48 us -> 1.38 us  [body(): jnp.concatenate([keys.reshape(tokens, groups, width), values.reshape(toke...]
    ppermute x2, starting transfers between devices: 6.36 us -> 2.48 us  [the longest x1 2.48 us: body(): lax.ppermute(kv, 'seq', [((i + 1) % count, i) for i in range(count)])]
  transfers between devices with their start and end apart: 4 -> 3, of which waited for: 3 -> 2; matrix products, arithmetic and copies ran while one was open for 7% -> 0% of each run, Pallas kernels for 0% -> 0%
where the time goes in v1:
time: 119 us
  blocking collectives  74.7 us (63%)
  waiting for transfers between devices  23.2 us (19%)
  Pallas kernels  9.58 us (8%)
  starting transfers between devices  9.09 us (8%)
  other arithmetic  1.38 us (1%)
    all_to_all x1, blocking collectives, body(): kv = lax.all_to_all(both, 'head', split_axis=1, concat_axis=0, tiled=True)  46.6 us
    all_to_all x1, blocking collectives, body(): lax.all_to_all(mixed, 'head', split_axis=0, concat_axis=1, tiled=True)  28.2 us
    all_to_all x1, waiting for transfers between devices, body(): q = lax.all_to_all(queries, 'head', split_axis=1, concat_axis=0, tiled=True)  20.3 us
    pallas_call x1, Pallas kernels, attend(): pl.pallas_call(functools.partial(attend_kernel, reach, tokens_all), out_s...  9.58 us
    all_to_all x1, starting transfers between devices, body(): q = lax.all_to_all(queries, 'head', split_axis=1, concat_axis=0, tiled=True)  6.61 us
    ppermute x1, waiting for transfers between devices, body(): left = lax.ppermute(kv, 'seq', [(i, (i + 1) % count) for i in range(count)])  2.96 us
    ppermute x1, starting transfers between devices, body(): lax.ppermute(kv, 'seq', [((i + 1) % count, i) for i in range(count)])  2.48 us
  transfers between devices with their start and end apart: 3, of which 2 were waited for; matrix products, arithmetic and copies ran while one was open for 0% of the time, Pallas kernels for 0%

profile of v1, /device:TPU:1, one launch (start us, length us, event | category | flops | bytes accessed | tf_op | source)
XLA Modules:
  0.0 119.0 jit_solution(5130843717230870793)
XLA Ops:
  0.0 1.4 %pad_maximum_fusion = bf16[8,64,1280]{2,0,1:T(8,128)(2,1)S(1)} fusion(bf16[8,64,640]{2,0,1:T(8,128)(2,1)} %bitcast.20, bf16[8,64,640]{2,0,1:T(8,128)(2,1)} %bitcast.21), kind=kLoop, calls=%fused_computation | loop fusion | flops 2621440 | bytes 2621440 | tf_op jit(solution)/shard_map/concatenate | solution.py:99
  1.4 46.6 %all_to_all.54 = bf16[8,64,1280]{2,0,1:T(8,128)(2,1)S(1)} all-to-all(bf16[8,64,1280]{2,0,1:T(8,128)(2,1)S(1)} %pad_maximum_fusion), channel_id=1, replica_groups=mesh['seq'=4,'head'=64] {'head'}, dimensions={1} | all-to-all | bytes 2621440 | tf_op jit(solution)/shard_map/all_to_all | solution.py:102
  47.9 0.0 copy-start.1
  47.9 0.0 copy-start
  47.9 2.5 %collective-permute-start.1 = (bf16[512,1280]{1,0:T(8,128)(2,1)S(1)}, bf16[512,1280]{1,0:T(8,128)(2,1)S(1)}, u32[]{:S(2)}, u32[]{:S(2)}) collective-permute-start(bf16[512,1280]{1,0:T(8,128)(2,1)S(1)} %bitcast.14), channel_id=1, source_target_pairs={{64,0},{128,64},{192,128},{0,192},{65,1},{129,65},{193,129},{1,193... | collective-permute-start | bytes 3932168 | tf_op jit(solution)/shard_map/ppermute | solution.py:105
  50.4 0.0 collective-permute-start
  50.4 6.6 %all-to-all-start = ((bf16[8,64,640]{2,0,1:T(8,128)(2,1)}), bf16[8,64,640]{2,0,1:T(8,128)(2,1)S(1)}, u32[]{:S(2)}, u32[]{:S(2)}) async-start(bf16[8,64,640]{2,0,1:T(8,128)(2,1)} %bitcast.22), calls=%async_computation | async-start | bytes 1310720 | tf_op jit(solution)/shard_map/all_to_all | solution.py:106
  57.1 0.0 copy-done.1
  57.1 0.1 copy.6.mask_ref
  57.1 20.3 %all-to-all-done = bf16[8,64,640]{2,0,1:T(8,128)(2,1)S(1)} async-done(((bf16[8,64,640]{2,0,1:T(8,128)(2,1)}), bf16[8,64,640]{2,0,1:T(8,128)(2,1)S(1)}, u32[]{:S(2)}, u32[]{:S(2)}) %all-to-all-start) | async-done | bytes 655392 | tf_op jit(solution)/shard_map/all_to_all | solution.py:106
  77.4 0.0 collective-permute-done.1.right_ref
  77.4 3.0 %collective-permute-done.left_ref = bf16[512,1280]{1,0:T(8,128)(2,1)} collective-permute-done((bf16[512,1280]{1,0:T(8,128)(2,1)S(1)}, bf16[512,1280]{1,0:T(8,128)(2,1)}, u32[]{:S(2)}, u32[]{:S(2)}) %collective-permute-start) | collective-permute-done | bytes 1310752 | tf_op jit(solution)/shard_map/ppermute | solution.py:104
  80.4 0.0 copy-done
  80.4 9.6 %shard_map.55 = bf16[512,640]{1,0:T(8,128)(2,1)S(1)} custom-call(s32[4]{0:T(128)S(1)} %copy-done, s32[1]{0:T(128)} %bitcast.first_ref, s32[1,16,9]{2,1,0:T(8,128)S(1)} %copy.6.mask_ref, bf16[512,640]{1,0:T(8,128)(2,1)S(1)} %bitcast.17, bf16[512,1280]{1,0:T(8,128)(2,1)S(1)} %bitcast.16, bf16[512,1280]{1,0:T(8,128)(2,1)} %collective-permute-done.left_ref, ...), custom_call_target="tpu_custom_call" | custom-call | flops 1500000000 | bytes 6000000 | tf_op jit(solution)/shard_map/pallas_call | solution.py:85
  90.0 28.2 %all_to_all.55 = bf16[64,8,640]{2,1,0:T(8,128)(2,1)S(1)} all-to-all(bf16[64,8,640]{2,1,0:T(8,128)(2,1)S(1)} %bitcast.18), channel_id=1, replica_groups=mesh['seq'=4,'head'=64] {'head'}, dimensions={0} | all-to-all | bytes 1310720 | tf_op jit(solution)/shard_map/all_to_all | solution.py:109
  118.1 0.8 copy.8
Async XLA Ops:
  47.9 9.1 %copy-start.1 = (s32[1,16,9]{1,0,2:T(1,128)S(1)}, s32[1,16,9]{1,0,2:T(1,128)}, u32[]{:S(2)}) copy-start(s32[1,16,9]{1,0,2:T(1,128)} %param.8) | copy-start | bytes 1732
  47.9 32.4 %copy-start = (s32[4]{0:T(128)S(1)}, s32[4]{0:T(128)}, u32[]{:S(2)}) copy-start(s32[4]{0:T(128)} %lengths.1) | copy-start | bytes 52
  47.9 29.5 %collective-permute-start.1 = (bf16[512,1280]{1,0:T(8,128)(2,1)S(1)}, bf16[512,1280]{1,0:T(8,128)(2,1)S(1)}, u32[]{:S(2)}, u32[]{:S(2)}) collective-permute-start(bf16[512,1280]{1,0:T(8,128)(2,1)S(1)} %bitcast.14), channel_id=1, source_target_pairs={{64,0},{128,64},{192,128},{0,192},{65,1},{129,65},{193,129},{1,193... | collective-permute-start | bytes 3932168 | tf_op jit(solution)/shard_map/ppermute | solution.py:105
  50.4 29.9 %collective-permute-start = (bf16[512,1280]{1,0:T(8,128)(2,1)S(1)}, bf16[512,1280]{1,0:T(8,128)(2,1)}, u32[]{:S(2)}, u32[]{:S(2)}) collective-permute-start(bf16[512,1280]{1,0:T(8,128)(2,1)S(1)} %bitcast.15), channel_id=1, source_target_pairs={{0,64},{64,128},{128,192},{192,0},{1,65},{65,129},{129,193},{193,1... | collective-permute-start | bytes 3932168 | tf_op jit(solution)/shard_map/ppermute | solution.py:104
  50.4 27.0 %all-to-all-start = ((bf16[8,64,640]{2,0,1:T(8,128)(2,1)}), bf16[8,64,640]{2,0,1:T(8,128)(2,1)S(1)}, u32[]{:S(2)}, u32[]{:S(2)}) async-start(bf16[8,64,640]{2,0,1:T(8,128)(2,1)} %bitcast.22), calls=%async_computation | async-start | bytes 1310720 | tf_op jit(solution)/shard_map/all_to_all | solution.py:106

commit v2 on v1

v2 whole, which is shorter than its diff:
```python
import functools

import jax
import jax.numpy as jnp
from jax import lax
from jax.experimental import pallas as pl
from jax.experimental.pallas import tpu as pltpu
from jax.sharding import PartitionSpec as P

HEAD_DIM = 128
BLOCK = 128
LOG2_E = 1.4426950408889634
neg_big = -1e30


def segment_of(positions, ends):
    seg = jnp.zeros_like(positions)
    for end in ends:
        seg = seg + (positions >= end).astype(jnp.int32)
    return seg


def mask_kernel(reach, tokens_all, lengths, first_ref, mask_ref, bias_ref):
    rows = bias_ref.shape[0]
    first = first_ref[0]
    ends = []
    total = lengths[0]
    for i in range(1, lengths.shape[0]):
        ends.append(total)
        total = total + lengths[i]
    for b in range(rows // BLOCK):
        q_pos = first + b * BLOCK + lax.broadcasted_iota(jnp.int32, (BLOCK, 1), 0)
        q_seg = segment_of(q_pos, ends)
        q_block = first // BLOCK + b
        for r in range(2 * reach + 1):
            k_pos = first + (b + r - reach) * BLOCK + lax.broadcasted_iota(jnp.int32, (1, BLOCK), 1)
            k_seg = segment_of(k_pos, ends)
            k_block = q_block + r - reach
            ok = (k_block >= 0) & (k_block < tokens_all // BLOCK)
            if r != reach:
                ok = ok & (mask_ref[0, q_block, r] == 1)
            k_seg = jnp.where(ok, k_seg, -1)
            bias_ref[b * BLOCK : (b + 1) * BLOCK, r * BLOCK : (r + 1) * BLOCK] = jnp.where(
                q_seg == k_seg, 0.0, neg_big
            )


def attend_kernel(bias_ref, q_ref, kv_ref, left_ref, right_ref, out_ref):
    rows, cols = q_ref.shape
    factor = LOG2_E / HEAD_DIM**0.5
    items = [(b, h) for b in range(rows // BLOCK) for h in range(cols // HEAD_DIM)]

    def here(b):
        return slice(b * BLOCK, (b + 1) * BLOCK)

    def parts(b):
        return (
            (left_ref, slice(b * BLOCK, rows)),
            (kv_ref, slice(0, rows)),
            (right_ref, slice(0, (b + 1) * BLOCK)),
        )

    def score(b, h):
        at = slice(h * HEAD_DIM, (h + 1) * HEAD_DIM)
        q = q_ref[here(b), at]
        products = [
            lax.dot_general(q, ref[part, at], (((1,), (1,)), ((), ())), preferred_element_type=jnp.float32)
            for ref, part in parts(b)
        ]
        return jnp.concatenate(products, axis=1) + bias_ref[here(b), :]

    def weigh(scores):
        row_max = jnp.max(scores, axis=1, keepdims=True)
        weights = jnp.exp2((scores - row_max) * factor)
        return weights.astype(jnp.bfloat16), jnp.sum(weights, axis=1, keepdims=True)

    def mix(b, h, weights, sums):
        at = slice(cols + h * HEAD_DIM, cols + (h + 1) * HEAD_DIM)
        mixed = jnp.zeros((BLOCK, HEAD_DIM), jnp.float32)
        seen = 0
        for ref, part in parts(b):
            width = part.stop - part.start
            mixed = mixed + jnp.dot(
                weights[:, seen : seen + width], ref[part, at], preferred_element_type=jnp.float32
            )
            seen += width
        out_ref[here(b), h * HEAD_DIM : (h + 1) * HEAD_DIM] = (mixed / sums).astype(jnp.bfloat16)

    scored = {0: score(*items[0])}
    weighed = {}
    for i in range(len(items) + 1):
        if i + 1 < len(items):
            scored[i + 1] = score(*items[i + 1])
        if i < len(items):
            weighed[i] = weigh(scored.pop(i))
        if i > 0:
            mix(*items[i - 1], *weighed.pop(i - 1))


smem = pl.BlockSpec(memory_space=pltpu.SMEM)
vmem = pl.BlockSpec(memory_space=pltpu.VMEM)


def mask_bias(prompt_lengths, first, block_mask, rows):
    span = block_mask.shape[2]
    return pl.pallas_call(
        functools.partial(mask_kernel, (span - 1) // 2, block_mask.shape[1] * BLOCK),
        out_shape=jax.ShapeDtypeStruct((rows, span * BLOCK), jnp.float32),
        in_specs=[smem, smem, smem],
        out_specs=vmem,
        compiler_params=pltpu.CompilerParams(vmem_limit_bytes=12 * 1024 * 1024),
        cost_estimate=pl.CostEstimate(flops=3000000, bytes_accessed=2400000, transcendentals=0),
    )(prompt_lengths, first, block_mask)


def attend(bias, q, kv, left, right):
    return pl.pallas_call(
        attend_kernel,
        out_shape=jax.ShapeDtypeStruct(q.shape, q.dtype),
        in_specs=[vmem] * 5,
        out_specs=vmem,
        compiler_params=pltpu.CompilerParams(vmem_limit_bytes=12 * 1024 * 1024),
        cost_estimate=pl.CostEstimate(flops=1500000000, bytes_accessed=6000000, transcendentals=3000000),
    )(bias, q, kv, left, right)


def body(queries, keys, values, block_mask, prompt_lengths):
    groups = lax.axis_size("head")
    tokens, cols = queries.shape
    width = cols // groups
    both = jnp.concatenate(
        [keys.reshape(tokens, groups, width), values.reshape(tokens, groups, width)], axis=2
    ).reshape(tokens, 2 * cols)
    kv = lax.all_to_all(both, "head", split_axis=1, concat_axis=0, tiled=True)
    count = lax.axis_size("seq")
    left = lax.ppermute(kv, "seq", [(i, (i + 1) % count) for i in range(count)])
    right = lax.ppermute(kv, "seq", [((i + 1) % count, i) for i in range(count)])
    q = lax.all_to_all(queries, "head", split_axis=1, concat_axis=0, tiled=True)
    first = (lax.axis_index("seq") * q.shape[0]).astype(jnp.int32).reshape(1)
    bias = mask_bias(prompt_lengths, first, block_mask, q.shape[0])
    mixed = attend(bias, q, kv, left, right)
    return lax.all_to_all(mixed, "head", split_axis=0, concat_axis=1, tiled=True)


def solution(mesh):
    placed = (
        P(("seq", "head"), None),
        P(("seq", "head"), None),
        P(("seq", "head"), None),
        P("head", None, None),
        P(),
    )
    return jax.shard_map(
        body, mesh=mesh, in_specs=placed, out_specs=P(("seq", "head"), None), check_vma=False
    )
```

time: 119 us -> 117 us (0.983)
  Pallas kernels: 9.58 us -> 7.61 us
    pallas_call x1 -> x2, Pallas kernels: 9.58 us -> 7.61 us  [the longest x1 6.67 us: attend(): pl.pallas_call(attend_kernel, out_shape=jax.ShapeDtypeStruct(q.shape, q.d...]
  transfers between devices with their start and end apart: 3 -> 3, of which waited for: 2 -> 2; matrix products, arithmetic and copies ran while one was open for 0% -> 0% of each run, Pallas kernels for 0% -> 1%
where the time goes in v2:
time: 117 us; the launch traced here: 116 us
  blocking collectives  74.8 us (64%)
  waiting for transfers between devices  22.5 us (19%)
  starting transfers between devices  9.09 us (8%)
  Pallas kernels  7.61 us (7%)
  other arithmetic  1.38 us (1%)
    all_to_all x1, blocking collectives, body(): kv = lax.all_to_all(both, 'head', split_axis=1, concat_axis=0, tiled=True)  46.7 us
    all_to_all x1, blocking collectives, body(): lax.all_to_all(mixed, 'head', split_axis=0, concat_axis=1, tiled=True)  28.2 us
    all_to_all x1, waiting for transfers between devices, body(): q = lax.all_to_all(queries, 'head', split_axis=1, concat_axis=0, tiled=True)  19.3 us
    pallas_call x1, Pallas kernels, attend(): pl.pallas_call(attend_kernel, out_shape=jax.ShapeDtypeStruct(q.shape, q.d...  6.67 us
    all_to_all x1, starting transfers between devices, body(): q = lax.all_to_all(queries, 'head', split_axis=1, concat_axis=0, tiled=True)  6.61 us
    ppermute x1, waiting for transfers between devices, body(): left = lax.ppermute(kv, 'seq', [(i, (i + 1) % count) for i in range(count)])  3.13 us
    ppermute x1, starting transfers between devices, body(): lax.ppermute(kv, 'seq', [((i + 1) % count, i) for i in range(count)])  2.48 us
  transfers between devices with their start and end apart: 3, of which 2 were waited for; matrix products, arithmetic and copies ran while one was open for 0% of the time, Pallas kernels for 1%

profile of v2, /device:TPU:1, one launch (start us, length us, event | category | flops | bytes accessed | tf_op | source)
XLA Modules:
  0.0 116.4 jit_solution(10444141499168000252)
XLA Ops:
  0.0 1.4 %pad_maximum_fusion = bf16[8,64,1280]{2,0,1:T(8,128)(2,1)S(1)} fusion(bf16[8,64,640]{2,0,1:T(8,128)(2,1)} %bitcast.17, bf16[8,64,640]{2,0,1:T(8,128)(2,1)} %bitcast.18), kind=kLoop, calls=%fused_computation | loop fusion | flops 2621440 | bytes 2621440 | tf_op jit(solution)/shard_map/concatenate | solution.py:131
  1.4 46.7 %all_to_all.54 = bf16[8,64,1280]{2,0,1:T(8,128)(2,1)} all-to-all(bf16[8,64,1280]{2,0,1:T(8,128)(2,1)S(1)} %pad_maximum_fusion), channel_id=1, replica_groups=mesh['seq'=4,'head'=64] {'head'}, dimensions={1} | all-to-all | bytes 2621440 | tf_op jit(solution)/shard_map/all_to_all | solution.py:134
  48.1 0.0 copy-start.1
  48.1 0.0 copy-start
  48.1 2.5 %collective-permute-start.1 = (bf16[512,1280]{1,0:T(8,128)(2,1)}, bf16[512,1280]{1,0:T(8,128)(2,1)}, u32[]{:S(2)}, u32[]{:S(2)}) collective-permute-start(bf16[512,1280]{1,0:T(8,128)(2,1)} %bitcast.7.kv_ref), channel_id=1, source_target_pairs={{64,0},{128,64},{192,128},{0,192},{65,1},{129,65},{193,129},{1,193... | collective-permute-start | bytes 3932168 | tf_op jit(solution)/shard_map/ppermute | solution.py:137
  50.5 0.0 collective-permute-start
  50.5 6.6 %all-to-all-start = ((bf16[8,64,640]{2,0,1:T(8,128)(2,1)}), bf16[8,64,640]{2,0,1:T(8,128)(2,1)S(1)}, u32[]{:S(2)}, u32[]{:S(2)}) async-start(bf16[8,64,640]{2,0,1:T(8,128)(2,1)} %bitcast.1), calls=%async_computation | async-start | bytes 1310720 | tf_op jit(solution)/shard_map/all_to_all | solution.py:138
  57.2 0.0 copy-done.1
  57.2 0.1 copy.6.mask_ref
  57.2 0.0 copy-done
  57.2 0.9 shard_map.55.bias_ref
  58.2 19.3 %all-to-all-done = bf16[8,64,640]{2,0,1:T(8,128)(2,1)S(1)} async-done(((bf16[8,64,640]{2,0,1:T(8,128)(2,1)}), bf16[8,64,640]{2,0,1:T(8,128)(2,1)S(1)}, u32[]{:S(2)}, u32[]{:S(2)}) %all-to-all-start) | async-done | bytes 655392 | tf_op jit(solution)/shard_map/all_to_all | solution.py:138
  77.5 0.0 collective-permute-done.1.right_ref
  77.6 3.1 %collective-permute-done.left_ref = bf16[512,1280]{1,0:T(8,128)(2,1)} collective-permute-done((bf16[512,1280]{1,0:T(8,128)(2,1)}, bf16[512,1280]{1,0:T(8,128)(2,1)}, u32[]{:S(2)}, u32[]{:S(2)}) %collective-permute-start) | collective-permute-done | bytes 1310752 | tf_op jit(solution)/shard_map/ppermute | solution.py:136
  80.7 6.7 %shard_map.56 = bf16[512,640]{1,0:T(8,128)(2,1)S(1)} custom-call(f32[512,1152]{1,0:T(8,128)S(1)} %shard_map.55.bias_ref, bf16[512,640]{1,0:T(8,128)(2,1)S(1)} %bitcast.14, bf16[512,1280]{1,0:T(8,128)(2,1)} %bitcast.7.kv_ref, bf16[512,1280]{1,0:T(8,128)(2,1)} %collective-permute-done.left_ref, bf16[512,1280]{1,0:T(8,128)(2,1)} %collective-permute-done.1.right_ref), custom_call_target="tpu_custom_call" | custom-call | flops 1500000000 | bytes 6000000 | tf_op jit(solution)/shard_map/pallas_call | solution.py:117
  87.4 28.2 %all_to_all.55 = bf16[64,8,640]{2,1,0:T(8,128)(2,1)S(1)} all-to-all(bf16[64,8,640]{2,1,0:T(8,128)(2,1)S(1)} %bitcast.15), channel_id=1, replica_groups=mesh['seq'=4,'head'=64] {'head'}, dimensions={0} | all-to-all | bytes 1310720 | tf_op jit(solution)/shard_map/all_to_all | solution.py:142
  115.5 0.8 copy.8
Async XLA Ops:
  48.1 9.1 %copy-start.1 = (s32[1,16,9]{1,0,2:T(1,128)S(1)}, s32[1,16,9]{1,0,2:T(1,128)}, u32[]{:S(2)}) copy-start(s32[1,16,9]{1,0,2:T(1,128)} %param.8) | copy-start | bytes 1732
  48.1 9.2 %copy-start = (s32[4]{0:T(128)S(1)}, s32[4]{0:T(128)}, u32[]{:S(2)}) copy-start(s32[4]{0:T(128)} %lengths.1) | copy-start | bytes 52
  48.1 29.5 %collective-permute-start.1 = (bf16[512,1280]{1,0:T(8,128)(2,1)}, bf16[512,1280]{1,0:T(8,128)(2,1)}, u32[]{:S(2)}, u32[]{:S(2)}) collective-permute-start(bf16[512,1280]{1,0:T(8,128)(2,1)} %bitcast.7.kv_ref), channel_id=1, source_target_pairs={{64,0},{128,64},{192,128},{0,192},{65,1},{129,65},{193,129},{1,193... | collective-permute-start | bytes 3932168 | tf_op jit(solution)/shard_map/ppermute | solution.py:137
  50.5 30.2 %collective-permute-start = (bf16[512,1280]{1,0:T(8,128)(2,1)}, bf16[512,1280]{1,0:T(8,128)(2,1)}, u32[]{:S(2)}, u32[]{:S(2)}) collective-permute-start(bf16[512,1280]{1,0:T(8,128)(2,1)} %bitcast.7.kv_ref), channel_id=1, source_target_pairs={{0,64},{64,128},{128,192},{192,0},{1,65},{65,129},{129,193},{193,1... | collective-permute-start | bytes 3932168 | tf_op jit(solution)/shard_map/ppermute | solution.py:136
  50.5 27.0 %all-to-all-start = ((bf16[8,64,640]{2,0,1:T(8,128)(2,1)}), bf16[8,64,640]{2,0,1:T(8,128)(2,1)S(1)}, u32[]{:S(2)}, u32[]{:S(2)}) async-start(bf16[8,64,640]{2,0,1:T(8,128)(2,1)} %bitcast.1), calls=%async_computation | async-start | bytes 1310720 | tf_op jit(solution)/shard_map/all_to_all | solution.py:138

commit v3 on v2

v3 whole, which is shorter than its diff:
```python
import functools

import jax
import jax.numpy as jnp
from jax import lax
from jax.experimental import pallas as pl
from jax.experimental.pallas import tpu as pltpu
from jax.sharding import PartitionSpec as P

HEAD_DIM = 128
BLOCK = 128
LOG2_E = 1.4426950408889634
neg_big = -1e30

smem = pl.BlockSpec(memory_space=pltpu.SMEM)
vmem = pl.BlockSpec(memory_space=pltpu.VMEM)


def segment_of(positions, ends):
    seg = jnp.zeros_like(positions)
    for end in ends:
        seg = seg + (positions >= end).astype(jnp.int32)
    return seg


def window_segments(reach, blocks_all, lengths, mask_ref, block):
    ends = []
    total = lengths[0]
    for i in range(1, lengths.shape[0]):
        ends.append(total)
        total = total + lengths[i]
    rows = segment_of(block * BLOCK + lax.broadcasted_iota(jnp.int32, (BLOCK, 1), 0), ends)
    keys = []
    for r in range(2 * reach + 1):
        other = block + r - reach
        ok = (other >= 0) & (other < blocks_all)
        if r != reach:
            ok = ok & (mask_ref[r, 0, block] == 1)
        pos = other * BLOCK + lax.broadcasted_iota(jnp.int32, (1, BLOCK), 1)
        keys.append(jnp.where(ok, segment_of(pos, ends), -1))
    return rows.astype(jnp.float32), jnp.concatenate(keys, axis=1).astype(jnp.float32)


def bias_of(rows, keys):
    return jnp.where(rows == keys, 0.0, neg_big)


def pipelined(items, score, weigh, mix):
    scored = {0: score(*items[0])}
    weighed = {}
    for i in range(len(items) + 1):
        if i + 1 < len(items):
            scored[i + 1] = score(*items[i + 1])
        if i < len(items):
            weighed[i] = weigh(*items[i], scored.pop(i))
        if i > 0:
            mix(*items[i - 1], *weighed.pop(i - 1))


def product(q, k):
    return lax.dot_general(q, k, (((1,), (1,)), ((), ())), preferred_element_type=jnp.float32)


def bias_kernel(reach, blocks_all, lengths, mask_ref, bias_ref):
    blocks = bias_ref.shape[0] // BLOCK
    first = lax.axis_index("seq") * blocks
    for b in range(blocks):
        bias_ref[b * BLOCK : (b + 1) * BLOCK, :] = bias_of(
            *window_segments(reach, blocks_all, lengths, mask_ref, first + b)
        )


def attend_kernel(bias_ref, q_ref, kv_ref, left_ref, right_ref, out_ref):
    rows, cols = q_ref.shape
    blocks = rows // BLOCK
    factor = LOG2_E / HEAD_DIM**0.5

    def here(b):
        return slice(b * BLOCK, (b + 1) * BLOCK)

    def parts(b):
        return (
            (left_ref, slice(b * BLOCK, rows)),
            (kv_ref, slice(0, rows)),
            (right_ref, slice(0, (b + 1) * BLOCK)),
        )

    def score(b, h):
        at = slice(h * HEAD_DIM, (h + 1) * HEAD_DIM)
        q = q_ref[here(b), at]
        return jnp.concatenate([product(q, ref[part, at]) for ref, part in parts(b)], axis=1) + bias_ref[here(b), :]

    def weigh(b, h, scores):
        row_max = jnp.max(scores, axis=1, keepdims=True)
        weights = jnp.exp2((scores - row_max) * factor)
        return weights.astype(jnp.bfloat16), jnp.sum(weights, axis=1, keepdims=True)

    def mix(b, h, weights, sums):
        at = slice(cols + h * HEAD_DIM, cols + (h + 1) * HEAD_DIM)
        mixed = jnp.zeros((BLOCK, HEAD_DIM), jnp.float32)
        seen = 0
        for ref, part in parts(b):
            width = part.stop - part.start
            mixed = mixed + jnp.dot(
                weights[:, seen : seen + width], ref[part, at], preferred_element_type=jnp.float32
            )
            seen += width
        out_ref[here(b), h * HEAD_DIM : (h + 1) * HEAD_DIM] = (mixed / sums).astype(jnp.bfloat16)

    pipelined([(b, h) for b in range(blocks) for h in range(cols // HEAD_DIM)], score, weigh, mix)


def mask_bias(prompt_lengths, block_mask, rows):
    _, blocks_all, span = block_mask.shape
    return pl.pallas_call(
        functools.partial(bias_kernel, (span - 1) // 2, blocks_all),
        out_shape=jax.ShapeDtypeStruct((rows, span * BLOCK), jnp.float32),
        in_specs=[smem, smem],
        out_specs=vmem,
        compiler_params=pltpu.CompilerParams(vmem_limit_bytes=4 * 1024 * 1024),
        cost_estimate=pl.CostEstimate(flops=3000000, bytes_accessed=2400000, transcendentals=0),
    )(prompt_lengths, block_mask.transpose(2, 0, 1))


def attend(bias, q, kv, left, right):
    return pl.pallas_call(
        attend_kernel,
        out_shape=jax.ShapeDtypeStruct(q.shape, q.dtype),
        in_specs=[vmem] * 5,
        out_specs=vmem,
        compiler_params=pltpu.CompilerParams(vmem_limit_bytes=12 * 1024 * 1024),
        cost_estimate=pl.CostEstimate(flops=1500000000, bytes_accessed=6000000, transcendentals=3000000),
    )(bias, q, kv, left, right)


def body(queries, keys, values, block_mask, prompt_lengths):
    groups = lax.axis_size("head")
    count = lax.axis_size("seq")
    tokens, cols = queries.shape
    width = cols // groups
    both = jnp.concatenate(
        [keys.reshape(tokens, groups, width), values.reshape(tokens, groups, width)], axis=2
    ).reshape(tokens, 2 * cols)
    kv = lax.all_to_all(both, "head", split_axis=1, concat_axis=0, tiled=True)
    left = lax.ppermute(kv, "seq", [(i, (i + 1) % count) for i in range(count)])
    right = lax.ppermute(kv, "seq", [((i + 1) % count, i) for i in range(count)])
    q = lax.all_to_all(queries, "head", split_axis=1, concat_axis=0, tiled=True)
    prompt_lengths, q = lax.optimization_barrier((prompt_lengths, q))
    bias = mask_bias(prompt_lengths, block_mask, q.shape[0])
    mixed = attend(bias, q, kv, left, right)
    return lax.all_to_all(mixed, "head", split_axis=0, concat_axis=1, tiled=True)


def solution(mesh):
    placed = (
        P(("seq", "head"), None),
        P(("seq", "head"), None),
        P(("seq", "head"), None),
        P("head", None, None),
        P(),
    )
    return jax.shard_map(
        body, mesh=mesh, in_specs=placed, out_specs=P(("seq", "head"), None), check_vma=False
    )
```

time: 117 us -> 114 us (0.974)
  blocking collectives: 74.8 us -> 102 us
  waiting for transfers between devices: 22.5 us -> 2.13 us
  starting transfers between devices: 9.09 us -> 2.48 us
  Pallas kernels: 7.61 us -> 5.52 us
    all_to_all x0 -> x1, blocking collectives: none -> 26.8 us  [body(): q = lax.all_to_all(queries, 'head', split_axis=1, concat_axis=0, tiled=True)]
    all_to_all x1 -> x0, waiting for transfers between devices: 19.3 us -> none  [body(): q = lax.all_to_all(queries, 'head', split_axis=1, concat_axis=0, tiled=True)]
    all_to_all x1 -> x0, starting transfers between devices: 6.61 us -> none  [body(): q = lax.all_to_all(queries, 'head', split_axis=1, concat_axis=0, tiled=True)]
    pallas_call x1, Pallas kernels: 6.67 us -> 4.59 us  [attend(): pl.pallas_call(attend_kernel, out_shape=jax.ShapeDtypeStruct(q.shape, q.d...]
  transfers between devices with their start and end apart: 3 -> 2, of which waited for: 2 -> 1; matrix products, arithmetic and copies ran while one was open for 0% -> 0% of each run, Pallas kernels for 1% -> 1%
where the time goes in v3:
time: 114 us
  blocking collectives  102 us (89%)
  Pallas kernels  5.52 us (5%)
  starting transfers between devices  2.48 us (2%)
  waiting for transfers between devices  2.13 us (2%)
  other arithmetic  1.38 us (1%)
    all_to_all x1, blocking collectives, body(): kv = lax.all_to_all(both, 'head', split_axis=1, concat_axis=0, tiled=True)  46.7 us
    all_to_all x1, blocking collectives, body(): lax.all_to_all(mixed, 'head', split_axis=0, concat_axis=1, tiled=True)  28.2 us
    all_to_all x1, blocking collectives, body(): q = lax.all_to_all(queries, 'head', split_axis=1, concat_axis=0, tiled=True)  26.8 us
    pallas_call x1, Pallas kernels, attend(): pl.pallas_call(attend_kernel, out_shape=jax.ShapeDtypeStruct(q.shape, q.d...  4.59 us
    ppermute x1, starting transfers between devices, body(): lax.ppermute(kv, 'seq', [((i + 1) % count, i) for i in range(count)])  2.48 us
  transfers between devices with their start and end apart: 2, of which 1 were waited for; matrix products, arithmetic and copies ran while one was open for 0% of the time, Pallas kernels for 1%

profile of v3, /device:TPU:1, one launch (start us, length us, event | category | flops | bytes accessed | tf_op | source)
XLA Modules:
  0.0 114.0 jit_solution(1948085083800067281)
XLA Ops:
  0.0 1.4 %pad_maximum_fusion = bf16[8,64,1280]{2,0,1:T(8,128)(2,1)S(1)} fusion(bf16[8,64,640]{2,0,1:T(8,128)(2,1)} %bitcast.21, bf16[8,64,640]{2,0,1:T(8,128)(2,1)} %bitcast.22), kind=kLoop, calls=%fused_computation | loop fusion | flops 2621440 | bytes 2621440 | tf_op jit(solution)/shard_map/concatenate | solution.py:141
  1.4 0.0 copy-start.2
  1.4 46.7 %all_to_all.54 = bf16[8,64,1280]{2,0,1:T(8,128)(2,1)S(1)} all-to-all(bf16[8,64,1280]{2,0,1:T(8,128)(2,1)S(1)} %pad_maximum_fusion), channel_id=1, replica_groups=mesh['seq'=4,'head'=64] {'head'}, dimensions={1} | all-to-all | bytes 2621440 | tf_op jit(solution)/shard_map/all_to_all | solution.py:144
  48.1 0.0 copy-start
  48.1 0.0 copy-start.1
  48.1 2.5 %collective-permute-start.1 = (bf16[512,1280]{1,0:T(8,128)(2,1)S(1)}, bf16[512,1280]{1,0:T(8,128)(2,1)S(1)}, u32[]{:S(2)}, u32[]{:S(2)}) collective-permute-start(bf16[512,1280]{1,0:T(8,128)(2,1)S(1)} %bitcast.14), channel_id=1, source_target_pairs={{64,0},{128,64},{192,128},{0,192},{65,1},{129,65},{193,129},{1,193... | collective-permute-start | bytes 3932168 | tf_op jit(solution)/shard_map/ppermute | solution.py:146
  50.6 0.0 collective-permute-start
  50.6 0.0 copy-done.2
  50.6 26.8 %all_to_all.55 = bf16[8,64,640]{2,0,1:T(8,128)(2,1)S(1)} all-to-all(bf16[8,64,640]{2,0,1:T(8,128)(2,1)S(1)} %bitcast.23), channel_id=1, replica_groups=mesh['seq'=4,'head'=64] {'head'}, dimensions={1} | all-to-all | bytes 1310720 | tf_op jit(solution)/shard_map/all_to_all | solution.py:147
  77.3 0.0 copy-done
  77.3 0.0 copy-done.1
  77.3 0.9 shard_map.55.bias_ref
  78.3 0.0 collective-permute-done.1.right_ref
  78.3 2.1 %collective-permute-done.left_ref = bf16[512,1280]{1,0:T(8,128)(2,1)S(1)} collective-permute-done((bf16[512,1280]{1,0:T(8,128)(2,1)S(1)}, bf16[512,1280]{1,0:T(8,128)(2,1)S(1)}, u32[]{:S(2)}, u32[]{:S(2)}) %collective-permute-start) | collective-permute-done | bytes 1310752 | tf_op jit(solution)/shard_map/ppermute | solution.py:145
  80.4 4.6 %shard_map.56 = bf16[512,640]{1,0:T(8,128)(2,1)S(1)} custom-call(f32[512,1152]{1,0:T(8,128)S(1)} %shard_map.55.bias_ref, bf16[512,640]{1,0:T(8,128)(2,1)S(1)} %bitcast.17, bf16[512,1280]{1,0:T(8,128)(2,1)S(1)} %bitcast.16, bf16[512,1280]{1,0:T(8,128)(2,1)S(1)} %collective-permute-done.left_ref, bf16[512,1280]{1,0:T(8,128)(2,1)S(1)} %collective-permute-done.1.right_ref), custom_call_target="tpu_custom_call" | custom-call | flops 1500000000 | bytes 6000000 | tf_op jit(solution)/shard_map/pallas_call | solution.py:126
  85.0 28.2 %all_to_all.56 = bf16[64,8,640]{2,1,0:T(8,128)(2,1)S(1)} all-to-all(bf16[64,8,640]{2,1,0:T(8,128)(2,1)S(1)} %bitcast.18), channel_id=1, replica_groups=mesh['seq'=4,'head'=64] {'head'}, dimensions={0} | all-to-all | bytes 1310720 | tf_op jit(solution)/shard_map/all_to_all | solution.py:151
  113.2 0.8 copy.7
Async XLA Ops:
  1.4 49.2 %copy-start.2 = (bf16[8,40960]{1,0:T(8,128)(2,1)S(1)}, bf16[8,40960]{1,0:T(8,128)(2,1)}, u32[]{:S(2)}) copy-start(bf16[8,40960]{1,0:T(8,128)(2,1)} %param.5) | copy-start | bytes 1966084
  48.1 29.2 %copy-start = (s32[1,16,9]{1,0,2:T(1,128)S(1)}, s32[1,16,9]{1,0,2:T(1,128)}, u32[]{:S(2)}) copy-start(s32[1,16,9]{1,0,2:T(1,128)} %param.8) | copy-start | bytes 1732
  48.1 29.2 %copy-start.1 = (s32[4]{0:T(128)S(1)}, s32[4]{0:T(128)}, u32[]{:S(2)}) copy-start(s32[4]{0:T(128)} %lengths) | copy-start | bytes 52
  48.1 30.2 %collective-permute-start.1 = (bf16[512,1280]{1,0:T(8,128)(2,1)S(1)}, bf16[512,1280]{1,0:T(8,128)(2,1)S(1)}, u32[]{:S(2)}, u32[]{:S(2)}) collective-permute-start(bf16[512,1280]{1,0:T(8,128)(2,1)S(1)} %bitcast.14), channel_id=1, source_target_pairs={{64,0},{128,64},{192,128},{0,192},{65,1},{129,65},{193,129},{1,193... | collective-permute-start | bytes 3932168 | tf_op jit(solution)/shard_map/ppermute | solution.py:146
  50.6 29.8 %collective-permute-start = (bf16[512,1280]{1,0:T(8,128)(2,1)S(1)}, bf16[512,1280]{1,0:T(8,128)(2,1)S(1)}, u32[]{:S(2)}, u32[]{:S(2)}) collective-permute-start(bf16[512,1280]{1,0:T(8,128)(2,1)S(1)} %bitcast.15), channel_id=1, source_target_pairs={{0,64},{64,128},{128,192},{192,0},{1,65},{65,129},{129,193},{193,1... | collective-permute-start | bytes 3932168 | tf_op jit(solution)/shard_map/ppermute | solution.py:145

commit v4 on v3

--- a/solution.py
+++ b/solution.py
@@ -61,16 +61,44 @@
     return lax.dot_general(q, k, (((1,), (1,)), ((), ())), preferred_element_type=jnp.float32)
 
 
-def bias_kernel(reach, blocks_all, lengths, mask_ref, bias_ref):
-    blocks = bias_ref.shape[0] // BLOCK
+def own_kernel(
+    reach, blocks_all, lengths, mask_ref, q_ref, kv_ref, bias_ref, max_ref, sum_ref, mixed_ref
+):
+    rows, cols = q_ref.shape
+    blocks = rows // BLOCK
+    factor = LOG2_E / HEAD_DIM**0.5
     first = lax.axis_index("seq") * blocks
+    biases = []
     for b in range(blocks):
-        bias_ref[b * BLOCK : (b + 1) * BLOCK, :] = bias_of(
-            *window_segments(reach, blocks_all, lengths, mask_ref, first + b)
-        )
+        bias = bias_of(*window_segments(reach, blocks_all, lengths, mask_ref, first + b))
+        start = (reach - b) * BLOCK
+        biases.append(bias[:, start : start + rows])
+        bias_ref[b * BLOCK : (b + 1) * BLOCK, :] = jnp.concatenate([bias[:, :start], bias[:, start + rows :]], axis=1)
+
+    def here(b):
+        return slice(b * BLOCK, (b + 1) * BLOCK)
+
+    def score(b, h):
+        at = slice(h * HEAD_DIM, (h + 1) * HEAD_DIM)
+        return product(q_ref[here(b), at], kv_ref[:, at]) + biases[b]
+
+    def weigh(b, h, scores):
+        at = slice(h * HEAD_DIM, (h + 1) * HEAD_DIM)
+        row_max = jnp.max(scores, axis=1, keepdims=True)
+        weights = jnp.exp2((scores - row_max) * factor)
+        max_ref[here(b), at] = jnp.broadcast_to(row_max, (BLOCK, HEAD_DIM))
+        sum_ref[here(b), at] = jnp.broadcast_to(jnp.sum(weights, axis=1, keepdims=True), (BLOCK, HEAD_DIM))
+        return (weights.astype(jnp.bfloat16),)
+
+    def mix(b, h, weights):
+        at = slice(h * HEAD_DIM, (h + 1) * HEAD_DIM)
+        v = kv_ref[:, cols + h * HEAD_DIM : cols + (h + 1) * HEAD_DIM]
+        mixed_ref[here(b), at] = jnp.dot(weights, v, preferred_element_type=jnp.float32)
+
+    pipelined([(b, h) for b in range(blocks) for h in range(cols // HEAD_DIM)], score, weigh, mix)
 
 
-def attend_kernel(bias_ref, q_ref, kv_ref, left_ref, right_ref, out_ref):
+def halo_kernel(bias_ref, max_ref, sum_ref, mixed_ref, q_ref, left_ref, right_ref, out_ref):
     rows, cols = q_ref.shape
     blocks = rows // BLOCK
     factor = LOG2_E / HEAD_DIM**0.5
@@ -78,59 +106,63 @@
     def here(b):
         return slice(b * BLOCK, (b + 1) * BLOCK)
 
-    def parts(b):
-        return (
-            (left_ref, slice(b * BLOCK, rows)),
-            (kv_ref, slice(0, rows)),
-            (right_ref, slice(0, (b + 1) * BLOCK)),
-        )
+    def sides(b):
+        return (left_ref, slice(b * BLOCK, rows)), (right_ref, slice(0, (b + 1) * BLOCK))
 
     def score(b, h):
         at = slice(h * HEAD_DIM, (h + 1) * HEAD_DIM)
         q = q_ref[here(b), at]
-        return jnp.concatenate([product(q, ref[part, at]) for ref, part in parts(b)], axis=1) + bias_ref[here(b), :]
+        return jnp.concatenate([product(q, ref[part, at]) for ref, part in sides(b)], axis=1) + bias_ref[here(b), :]
 
     def weigh(b, h, scores):
-        row_max = jnp.max(scores, axis=1, keepdims=True)
-        weights = jnp.exp2((scores - row_max) * factor)
-        return weights.astype(jnp.bfloat16), jnp.sum(weights, axis=1, keepdims=True)
+        at = slice(h * HEAD_DIM, (h + 1) * HEAD_DIM)
+        own_max = max_ref[here(b), at]
+        row_max = jnp.maximum(own_max, jnp.max(scores, axis=1, keepdims=True))
+        share = jnp.exp2((own_max - row_max) * factor)
+        copies = scores.shape[1] // HEAD_DIM
+        weights = jnp.exp2((scores - jnp.concatenate([row_max] * copies, axis=1)) * factor)
+        sums = jnp.sum(weights, axis=1, keepdims=True) + share * sum_ref[here(b), at]
+        return weights.astype(jnp.bfloat16), share, sums
 
-    def mix(b, h, weights, sums):
-        at = slice(cols + h * HEAD_DIM, cols + (h + 1) * HEAD_DIM)
-        mixed = jnp.zeros((BLOCK, HEAD_DIM), jnp.float32)
+    def mix(b, h, weights, share, sums):
+        at = slice(h * HEAD_DIM, (h + 1) * HEAD_DIM)
+        v_at = slice(cols + h * HEAD_DIM, cols + (h + 1) * HEAD_DIM)
+        mixed = mixed_ref[here(b), at] * share
         seen = 0
-        for ref, part in parts(b):
+        for ref, part in sides(b):
             width = part.stop - part.start
             mixed = mixed + jnp.dot(
-                weights[:, seen : seen + width], ref[part, at], preferred_element_type=jnp.float32
+                weights[:, seen : seen + width], ref[part, v_at], preferred_element_type=jnp.float32
             )
             seen += width
-        out_ref[here(b), h * HEAD_DIM : (h + 1) * HEAD_DIM] = (mixed / sums).astype(jnp.bfloat16)
+        out_ref[here(b), at] = (mixed / sums).astype(jnp.bfloat16)
 
     pipelined([(b, h) for b in range(blocks) for h in range(cols // HEAD_DIM)], score, weigh, mix)
 
 
-def mask_bias(prompt_lengths, block_mask, rows):
+def attend_own(prompt_lengths, block_mask, q, kv):
+    rows, cols = q.shape
     _, blocks_all, span = block_mask.shape
+    part = jax.ShapeDtypeStruct((rows, cols), jnp.float32)
     return pl.pallas_call(
-        functools.partial(bias_kernel, (span - 1) // 2, blocks_all),
-        out_shape=jax.ShapeDtypeStruct((rows, span * BLOCK), jnp.float32),
-        in_specs=[smem, smem],
-        out_specs=vmem,
-        compiler_params=pltpu.CompilerParams(vmem_limit_bytes=4 * 1024 * 1024),
-        cost_estimate=pl.CostEstimate(flops=3000000, bytes_accessed=2400000, transcendentals=0),
-    )(prompt_lengths, block_mask.transpose(2, 0, 1))
+        functools.partial(own_kernel, (span - 1) // 2, blocks_all),
+        out_shape=(jax.ShapeDtypeStruct((rows, span * BLOCK - rows), jnp.float32), part, part, part),
+        in_specs=[smem, smem, vmem, vmem],
+        out_specs=[vmem] * 4,
+        compiler_params=pltpu.CompilerParams(vmem_limit_bytes=12 * 1024 * 1024),
+        cost_estimate=pl.CostEstimate(flops=1000, bytes_accessed=1000, transcendentals=0),
+    )(prompt_lengths, block_mask.transpose(2, 0, 1), q, kv)
 
 
-def attend(bias, q, kv, left, right):
+def attend_halo(own, q, left, right):
     return pl.pallas_call(
-        attend_kernel,
+        halo_kernel,
         out_shape=jax.ShapeDtypeStruct(q.shape, q.dtype),
-        in_specs=[vmem] * 5,
+        in_specs=[vmem] * 7,
         out_specs=vmem,
         compiler_params=pltpu.CompilerParams(vmem_limit_bytes=12 * 1024 * 1024),
-        cost_estimate=pl.CostEstimate(flops=1500000000, bytes_accessed=6000000, transcendentals=3000000),
-    )(bias, q, kv, left, right)
+        cost_estimate=pl.CostEstimate(flops=900000000, bytes_accessed=4000000, transcendentals=1600000),
+    )(*own, q, left, right)
 
 
 def body(queries, keys, values, block_mask, prompt_lengths):
@@ -146,8 +178,8 @@
     right = lax.ppermute(kv, "seq", [((i + 1) % count, i) for i in range(count)])
     q = lax.all_to_all(queries, "head", split_axis=1, concat_axis=0, tiled=True)
     prompt_lengths, q = lax.optimization_barrier((prompt_lengths, q))
-    bias = mask_bias(prompt_lengths, block_mask, q.shape[0])
-    mixed = attend(bias, q, kv, left, right)
+    own = attend_own(prompt_lengths, block_mask, q, kv)
+    mixed = attend_halo(own, q, left, right)
     return lax.all_to_all(mixed, "head", split_axis=0, concat_axis=1, tiled=True)
 
 

time: 114 us -> 113 us (level)
  waiting for transfers between devices: 2.13 us -> 0.01 us
    ppermute x1, waiting for transfers between devices: 2.13 us -> 0.01 us  [body(): left = lax.ppermute(kv, 'seq', [(i, (i + 1) % count) for i in range(count)])]
  transfers between devices with their start and end apart: 2 -> 2, of which waited for: 1 -> 0; matrix products, arithmetic and copies ran while one was open for 0% -> 0% of each run, Pallas kernels for 1% -> 3%
where the time goes in v4:
time: 113 us
  blocking collectives  102 us (90%)
  Pallas kernels  6.34 us (6%)
  starting transfers between devices  2.48 us (2%)
  other arithmetic  1.38 us (1%)
    all_to_all x1, blocking collectives, body(): kv = lax.all_to_all(both, 'head', split_axis=1, concat_axis=0, tiled=True)  46.7 us
    all_to_all x1, blocking collectives, body(): lax.all_to_all(mixed, 'head', split_axis=0, concat_axis=1, tiled=True)  28.1 us
    all_to_all x1, blocking collectives, body(): q = lax.all_to_all(queries, 'head', split_axis=1, concat_axis=0, tiled=True)  26.8 us
    pallas_call x1, Pallas kernels, attend_halo(): pl.pallas_call(halo_kernel, out_shape=jax.ShapeDtypeStruct(q.shape, q.dty...  3.2 us
    pallas_call x1, Pallas kernels, attend_own(): pl.pallas_call(functools.partial(own_kernel, (span - 1) // 2, blocks_all)...  3.14 us
    ppermute x1, starting transfers between devices, body(): lax.ppermute(kv, 'seq', [((i + 1) % count, i) for i in range(count)])  2.48 us
  transfers between devices with their start and end apart: 2, of which 0 were waited for; matrix products, arithmetic and copies ran while one was open for 0% of the time, Pallas kernels for 3%

profile of v4, /device:TPU:1, one launch (start us, length us, event | category | flops | bytes accessed | tf_op | source)
XLA Modules:
  0.0 112.6 jit_solution(10458807365886772378)
XLA Ops:
  0.0 1.4 %pad_maximum_fusion = bf16[8,64,1280]{2,0,1:T(8,128)(2,1)S(1)} fusion(bf16[8,64,640]{2,0,1:T(8,128)(2,1)} %bitcast.22, bf16[8,64,640]{2,0,1:T(8,128)(2,1)} %bitcast.23), kind=kLoop, calls=%fused_computation | loop fusion | flops 2621440 | bytes 2621440 | tf_op jit(solution)/shard_map/concatenate | solution.py:173
  1.4 0.0 copy-start.2
  1.4 46.7 %all_to_all.54 = bf16[8,64,1280]{2,0,1:T(8,128)(2,1)S(1)} all-to-all(bf16[8,64,1280]{2,0,1:T(8,128)(2,1)S(1)} %pad_maximum_fusion), channel_id=1, replica_groups=mesh['seq'=4,'head'=64] {'head'}, dimensions={1} | all-to-all | bytes 2621440 | tf_op jit(solution)/shard_map/all_to_all | solution.py:176
  48.1 0.0 copy-start
  48.1 0.0 copy-start.1
  48.1 2.5 %collective-permute-start.1 = (bf16[512,1280]{1,0:T(8,128)(2,1)S(1)}, bf16[512,1280]{1,0:T(8,128)(2,1)S(1)}, u32[]{:S(2)}, u32[]{:S(2)}) collective-permute-start(bf16[512,1280]{1,0:T(8,128)(2,1)S(1)} %bitcast.16), channel_id=1, source_target_pairs={{64,0},{128,64},{192,128},{0,192},{65,1},{129,65},{193,129},{1,193... | collective-permute-start | bytes 3932168 | tf_op jit(solution)/shard_map/ppermute | solution.py:178
  50.6 0.0 collective-permute-start
  50.6 0.0 copy-done.2
  50.6 26.8 %all_to_all.55 = bf16[8,64,640]{2,0,1:T(8,128)(2,1)S(1)} all-to-all(bf16[8,64,640]{2,0,1:T(8,128)(2,1)S(1)} %bitcast.24), channel_id=1, replica_groups=mesh['seq'=4,'head'=64] {'head'}, dimensions={1} | all-to-all | bytes 1310720 | tf_op jit(solution)/shard_map/all_to_all | solution.py:179
  77.3 0.0 copy-done
  77.3 0.0 copy-done.1
  77.3 3.1 %shard_map.55 = (f32[512,640]{1,0:T(8,128)S(1)}, f32[512,640]{1,0:T(8,128)S(1)}, f32[512,640]{1,0:T(8,128)S(1)}, f32[512,640]{1,0:T(8,128)S(1)}) custom-call(s32[4]{0:T(128)S(1)} %copy-done.1, s32[9,1,16]{2,1,0:T(1,128)S(1)} %bitcast.20, bf16[512,640]{1,0:T(8,128)(2,1)S(1)} %bitcast.14, bf16[512,1280]{1,0:T(8,128)(2,1)S(1)} %bitcast.18), custom_call_target="tpu_custom_call" | custom-call | flops 1000 | bytes 1000 | tf_op jit(solution)/shard_map/pallas_call | solution.py:147
  80.5 0.0 collective-permute-done.1.right_ref
  80.5 0.0 collective-permute-done.left_ref
  80.5 3.2 %shard_map.56 = bf16[512,640]{1,0:T(8,128)(2,1)S(1)} custom-call(f32[512,640]{1,0:T(8,128)S(1)} %get-tuple-element.13.bias_ref, f32[512,640]{1,0:T(8,128)S(1)} %get-tuple-element.14.max_ref, f32[512,640]{1,0:T(8,128)S(1)} %get-tuple-element.15.sum_ref, f32[512,640]{1,0:T(8,128)S(1)} %get-tuple-element.16.mixed_ref, bf16[512,640]{1,0:T(8,128)(2,1)S(1)} %bitcast.15, ...), custom_call_target="tpu_custom_call" | custom-call | flops 900000000 | bytes 4000000 | tf_op jit(solution)/shard_map/pallas_call | solution.py:158
  83.7 28.1 %all_to_all.56 = bf16[64,8,640]{2,1,0:T(8,128)(2,1)S(1)} all-to-all(bf16[64,8,640]{2,1,0:T(8,128)(2,1)S(1)} %bitcast.19), channel_id=1, replica_groups=mesh['seq'=4,'head'=64] {'head'}, dimensions={0} | all-to-all | bytes 1310720 | tf_op jit(solution)/shard_map/all_to_all | solution.py:183
  111.8 0.8 copy.7
Async XLA Ops:
  1.4 49.2 %copy-start.2 = (bf16[8,40960]{1,0:T(8,128)(2,1)S(1)}, bf16[8,40960]{1,0:T(8,128)(2,1)}, u32[]{:S(2)}) copy-start(bf16[8,40960]{1,0:T(8,128)(2,1)} %param.5) | copy-start | bytes 1966084
  48.1 29.2 %copy-start = (s32[1,16,9]{1,0,2:T(1,128)S(1)}, s32[1,16,9]{1,0,2:T(1,128)}, u32[]{:S(2)}) copy-start(s32[1,16,9]{1,0,2:T(1,128)} %param.8) | copy-start | bytes 1732
  48.1 29.2 %copy-start.1 = (s32[4]{0:T(128)S(1)}, s32[4]{0:T(128)}, u32[]{:S(2)}) copy-start(s32[4]{0:T(128)} %lengths) | copy-start | bytes 52
  48.1 32.4 %collective-permute-start.1 = (bf16[512,1280]{1,0:T(8,128)(2,1)S(1)}, bf16[512,1280]{1,0:T(8,128)(2,1)S(1)}, u32[]{:S(2)}, u32[]{:S(2)}) collective-permute-start(bf16[512,1280]{1,0:T(8,128)(2,1)S(1)} %bitcast.16), channel_id=1, source_target_pairs={{64,0},{128,64},{192,128},{0,192},{65,1},{129,65},{193,129},{1,193... | collective-permute-start | bytes 3932168 | tf_op jit(solution)/shard_map/ppermute | solution.py:178
  50.6 29.9 %collective-permute-start = (bf16[512,1280]{1,0:T(8,128)(2,1)S(1)}, bf16[512,1280]{1,0:T(8,128)(2,1)S(1)}, u32[]{:S(2)}, u32[]{:S(2)}) collective-permute-start(bf16[512,1280]{1,0:T(8,128)(2,1)S(1)} %bitcast.17), channel_id=1, source_target_pairs={{0,64},{64,128},{128,192},{192,0},{1,65},{65,129},{129,193},{193,1... | collective-permute-start | bytes 3932168 | tf_op jit(solution)/shard_map/ppermute | solution.py:177

commit v5 on v4

--- a/solution.py
+++ b/solution.py
@@ -46,11 +46,11 @@
 
 
 def pipelined(items, score, weigh, mix):
-    scored = {0: score(*items[0])}
+    scored = {0: score(*items[0]), 1: score(*items[1])}
     weighed = {}
     for i in range(len(items) + 1):
-        if i + 1 < len(items):
-            scored[i + 1] = score(*items[i + 1])
+        if i + 2 < len(items):
+            scored[i + 2] = score(*items[i + 2])
         if i < len(items):
             weighed[i] = weigh(*items[i], scored.pop(i))
         if i > 0:
@@ -98,7 +98,20 @@
     pipelined([(b, h) for b in range(blocks) for h in range(cols // HEAD_DIM)], score, weigh, mix)
 
 
-def halo_kernel(bias_ref, max_ref, sum_ref, mixed_ref, q_ref, left_ref, right_ref, out_ref):
+def halo_kernel(*refs):
+    *others, one_ref, two_ref, out_ref = refs
+    odd = lax.axis_index("head") % 2
+
+    @pl.when(odd == 0)
+    def _():
+        add_halo(*others, one_ref, two_ref, out_ref)
+
+    @pl.when(odd == 1)
+    def _():
+        add_halo(*others, two_ref, one_ref, out_ref)
+
+
+def add_halo(bias_ref, max_ref, sum_ref, mixed_ref, q_ref, left_ref, right_ref, out_ref):
     rows, cols = q_ref.shape
     blocks = rows // BLOCK
     factor = LOG2_E / HEAD_DIM**0.5
@@ -174,12 +187,22 @@
         [keys.reshape(tokens, groups, width), values.reshape(tokens, groups, width)], axis=2
     ).reshape(tokens, 2 * cols)
     kv = lax.all_to_all(both, "head", split_axis=1, concat_axis=0, tiled=True)
-    left = lax.ppermute(kv, "seq", [(i, (i + 1) % count) for i in range(count)])
-    right = lax.ppermute(kv, "seq", [((i + 1) % count, i) for i in range(count)])
+    one, two = (
+        lax.ppermute(
+            kv,
+            ("seq", "head"),
+            [
+                (i * groups + g, (i + step * (1 - 2 * (g % 2))) % count * groups + g)
+                for i in range(count)
+                for g in range(groups)
+            ],
+        )
+        for step in (1, -1)
+    )
     q = lax.all_to_all(queries, "head", split_axis=1, concat_axis=0, tiled=True)
     prompt_lengths, q = lax.optimization_barrier((prompt_lengths, q))
     own = attend_own(prompt_lengths, block_mask, q, kv)
-    mixed = attend_halo(own, q, left, right)
+    mixed = attend_halo(own, q, one, two)
     return lax.all_to_all(mixed, "head", split_axis=0, concat_axis=1, tiled=True)
 
 

time: 113 us -> 111 us (0.982)
  blocking collectives: 102 us -> 99.3 us
    all_to_all x1, blocking collectives: 28.1 us -> 26 us  [body(): lax.all_to_all(mixed, 'head', split_axis=0, concat_axis=1, tiled=True)]
where the time goes in v5:
time: 111 us; the launch traced here: 110 us
  blocking collectives  99.3 us (89%)
  Pallas kernels  6.08 us (5%)
  starting transfers between devices  2.68 us (2%)
  other arithmetic  1.38 us (1%)
    all_to_all x1, blocking collectives, body(): kv = lax.all_to_all(both, 'head', split_axis=1, concat_axis=0, tiled=True)  46.7 us
    all_to_all x1, blocking collectives, body(): q = lax.all_to_all(queries, 'head', split_axis=1, concat_axis=0, tiled=True)  26.6 us
    all_to_all x1, blocking collectives, body(): lax.all_to_all(mixed, 'head', split_axis=0, concat_axis=1, tiled=True)  26 us
    pallas_call x1, Pallas kernels, attend_halo(): pl.pallas_call(halo_kernel, out_shape=jax.ShapeDtypeStruct(q.shape, q.dty...  3.06 us
    pallas_call x1, Pallas kernels, attend_own(): pl.pallas_call(functools.partial(own_kernel, (span - 1) // 2, blocks_all)...  3.02 us
    ppermute x2, starting transfers between devices, body(): lax.ppermute(kv, ('seq', 'head'), [(i * groups + g, (i + step * (1 - 2 *...  2.68 us
  transfers between devices with their start and end apart: 2, of which 0 were waited for; matrix products, arithmetic and copies ran while one was open for 0% of the time, Pallas kernels for 3%

profile of v5, /device:TPU:1, one launch (start us, length us, event | category | flops | bytes accessed | tf_op | source)
XLA Modules:
  0.0 110.3 jit_solution(18307466776521705609)
XLA Ops:
  0.0 1.4 %pad_maximum_fusion = bf16[8,64,1280]{2,0,1:T(8,128)(2,1)S(1)} fusion(bf16[8,64,640]{2,0,1:T(8,128)(2,1)} %bitcast.22, bf16[8,64,640]{2,0,1:T(8,128)(2,1)} %bitcast.23), kind=kLoop, calls=%fused_computation | loop fusion | flops 2621440 | bytes 2621440 | tf_op jit(solution)/shard_map/concatenate | solution.py:186
  1.4 0.0 copy-start.2
  1.4 46.7 %all_to_all.54 = bf16[8,64,1280]{2,0,1:T(8,128)(2,1)S(1)} all-to-all(bf16[8,64,1280]{2,0,1:T(8,128)(2,1)S(1)} %pad_maximum_fusion), channel_id=1, replica_groups=mesh['seq'=4,'head'=64] {'head'}, dimensions={1} | all-to-all | bytes 2621440 | tf_op jit(solution)/shard_map/all_to_all | solution.py:189
  48.1 0.0 copy-start
  48.1 0.0 copy-start.1
  48.1 1.2 %collective-permute-start.1 = (bf16[512,1280]{1,0:T(8,128)(2,1)S(1)}, bf16[512,1280]{1,0:T(8,128)(2,1)S(1)}, u32[]{:S(2)}, u32[]{:S(2)}) collective-permute-start(bf16[512,1280]{1,0:T(8,128)(2,1)S(1)} %bitcast.16), channel_id=1, source_target_pairs={{0,192},{1,65},{2,194},{3,67},{4,196},{5,69},{6,198},{7,71},{8,200... | collective-permute-start | bytes 3932168 | tf_op jit(solution)/shard_map/ppermute | solution.py:191
  49.3 1.5 %collective-permute-start = (bf16[512,1280]{1,0:T(8,128)(2,1)S(1)}, bf16[512,1280]{1,0:T(8,128)(2,1)S(1)}, u32[]{:S(2)}, u32[]{:S(2)}) collective-permute-start(bf16[512,1280]{1,0:T(8,128)(2,1)S(1)} %bitcast.17), channel_id=1, source_target_pairs={{0,64},{1,193},{2,66},{3,195},{4,68},{5,197},{6,70},{7,199},{8,72}... | collective-permute-start | bytes 3932168 | tf_op jit(solution)/shard_map/ppermute | solution.py:191
  50.8 0.0 copy-done.2
  50.8 26.6 %all_to_all.55 = bf16[8,64,640]{2,0,1:T(8,128)(2,1)S(1)} all-to-all(bf16[8,64,640]{2,0,1:T(8,128)(2,1)S(1)} %bitcast.24), channel_id=1, replica_groups=mesh['seq'=4,'head'=64] {'head'}, dimensions={1} | all-to-all | bytes 1310720 | tf_op jit(solution)/shard_map/all_to_all | solution.py:202
  77.3 0.0 copy-done
  77.3 0.0 copy-done.1
  77.3 3.0 %shard_map.55 = (f32[512,640]{1,0:T(8,128)S(1)}, f32[512,640]{1,0:T(8,128)S(1)}, f32[512,640]{1,0:T(8,128)S(1)}, f32[512,640]{1,0:T(8,128)S(1)}) custom-call(s32[4]{0:T(128)S(1)} %copy-done.1, s32[9,1,16]{2,1,0:T(1,128)S(1)} %bitcast.20, bf16[512,640]{1,0:T(8,128)(2,1)S(1)} %bitcast.14, bf16[512,1280]{1,0:T(8,128)(2,1)S(1)} %bitcast.18), custom_call_target="tpu_custom_call" | custom-call | flops 1000 | bytes 1000 | tf_op jit(solution)/shard_map/pallas_call | solution.py:160
  80.4 0.0 collective-permute-done.1.refs_6_
  80.4 0.0 collective-permute-done.refs_5_
  80.4 3.1 %shard_map.56 = bf16[512,640]{1,0:T(8,128)(2,1)S(1)} custom-call(f32[512,640]{1,0:T(8,128)S(1)} %get-tuple-element.13.refs_0_, f32[512,640]{1,0:T(8,128)S(1)} %get-tuple-element.14.refs_1_, f32[512,640]{1,0:T(8,128)S(1)} %get-tuple-element.15.refs_2_, f32[512,640]{1,0:T(8,128)S(1)} %get-tuple-element.16.refs_3_, bf16[512,640]{1,0:T(8,128)(2,1)S(1)} %bitcast.15, ...), custom_call_target="tpu_custom_call" | custom-call | flops 900000000 | bytes 4000000 | tf_op jit(solution)/shard_map/pallas_call | solution.py:171
  83.5 26.0 %all_to_all.56 = bf16[64,8,640]{2,1,0:T(8,128)(2,1)S(1)} all-to-all(bf16[64,8,640]{2,1,0:T(8,128)(2,1)S(1)} %bitcast.19), channel_id=1, replica_groups=mesh['seq'=4,'head'=64] {'head'}, dimensions={0} | all-to-all | bytes 1310720 | tf_op jit(solution)/shard_map/all_to_all | solution.py:206
  109.5 0.8 copy.7
Async XLA Ops:
  1.4 49.4 %copy-start.2 = (bf16[8,40960]{1,0:T(8,128)(2,1)S(1)}, bf16[8,40960]{1,0:T(8,128)(2,1)}, u32[]{:S(2)}) copy-start(bf16[8,40960]{1,0:T(8,128)(2,1)} %param.5) | copy-start | bytes 1966084
  48.1 29.2 %copy-start = (s32[1,16,9]{1,0,2:T(1,128)S(1)}, s32[1,16,9]{1,0,2:T(1,128)}, u32[]{:S(2)}) copy-start(s32[1,16,9]{1,0,2:T(1,128)} %param.8) | copy-start | bytes 1732
  48.1 29.2 %copy-start.1 = (s32[4]{0:T(128)S(1)}, s32[4]{0:T(128)}, u32[]{:S(2)}) copy-start(s32[4]{0:T(128)} %lengths) | copy-start | bytes 52
  48.1 32.3 %collective-permute-start.1 = (bf16[512,1280]{1,0:T(8,128)(2,1)S(1)}, bf16[512,1280]{1,0:T(8,128)(2,1)S(1)}, u32[]{:S(2)}, u32[]{:S(2)}) collective-permute-start(bf16[512,1280]{1,0:T(8,128)(2,1)S(1)} %bitcast.16), channel_id=1, source_target_pairs={{0,192},{1,65},{2,194},{3,67},{4,196},{5,69},{6,198},{7,71},{8,200... | collective-permute-start | bytes 3932168 | tf_op jit(solution)/shard_map/ppermute | solution.py:191
  49.3 31.1 %collective-permute-start = (bf16[512,1280]{1,0:T(8,128)(2,1)S(1)}, bf16[512,1280]{1,0:T(8,128)(2,1)S(1)}, u32[]{:S(2)}, u32[]{:S(2)}) collective-permute-start(bf16[512,1280]{1,0:T(8,128)(2,1)S(1)} %bitcast.17), channel_id=1, source_target_pairs={{0,64},{1,193},{2,66},{3,195},{4,68},{5,197},{6,70},{7,199},{8,72}... | collective-permute-start | bytes 3932168 | tf_op jit(solution)/shard_map/ppermute | solution.py:191

commit v6 on v5

--- a/solution.py
+++ b/solution.py
@@ -10,7 +10,7 @@
 HEAD_DIM = 128
 BLOCK = 128
 LOG2_E = 1.4426950408889634
-neg_big = -1e30
+LARGEST = 3.4028234663852886e38
 
 smem = pl.BlockSpec(memory_space=pltpu.SMEM)
 vmem = pl.BlockSpec(memory_space=pltpu.VMEM)
@@ -41,8 +41,8 @@
     return rows.astype(jnp.float32), jnp.concatenate(keys, axis=1).astype(jnp.float32)
 
 
-def bias_of(rows, keys):
-    return jnp.where(rows == keys, 0.0, neg_big)
+def limit_of(rows, keys):
+    return jnp.where(rows == keys, LARGEST, -LARGEST)
 
 
 def pipelined(items, score, weigh, mix):
@@ -62,40 +62,38 @@
 
 
 def own_kernel(
-    reach, blocks_all, lengths, mask_ref, q_ref, kv_ref, bias_ref, max_ref, sum_ref, mixed_ref
+    reach, blocks_all, lengths, mask_ref, q_ref, kv_ref, limit_ref, max_ref, sum_ref, mixed_ref
 ):
     rows, cols = q_ref.shape
     blocks = rows // BLOCK
     factor = LOG2_E / HEAD_DIM**0.5
     first = lax.axis_index("seq") * blocks
-    biases = []
+    limits = []
     for b in range(blocks):
-        bias = bias_of(*window_segments(reach, blocks_all, lengths, mask_ref, first + b))
+        limit = limit_of(*window_segments(reach, blocks_all, lengths, mask_ref, first + b))
         start = (reach - b) * BLOCK
-        biases.append(bias[:, start : start + rows])
-        bias_ref[b * BLOCK : (b + 1) * BLOCK, :] = jnp.concatenate([bias[:, :start], bias[:, start + rows :]], axis=1)
-
-    def here(b):
-        return slice(b * BLOCK, (b + 1) * BLOCK)
-
-    def score(b, h):
-        at = slice(h * HEAD_DIM, (h + 1) * HEAD_DIM)
-        return product(q_ref[here(b), at], kv_ref[:, at]) + biases[b]
-
-    def weigh(b, h, scores):
+        limits.append(limit[:, start : start + rows])
+        limit_ref[b * BLOCK : (b + 1) * BLOCK, :] = jnp.concatenate([limit[:, :start], limit[:, start + rows :]], axis=1)
+
+    limits = jnp.concatenate(limits, axis=0)
+
+    def score(h):
+        at = slice(h * HEAD_DIM, (h + 1) * HEAD_DIM)
+        return jnp.minimum(product(q_ref[:, at], kv_ref[:, at]), limits)
+
+    def weigh(h, scores):
         at = slice(h * HEAD_DIM, (h + 1) * HEAD_DIM)
         row_max = jnp.max(scores, axis=1, keepdims=True)
         weights = jnp.exp2((scores - row_max) * factor)
-        max_ref[here(b), at] = jnp.broadcast_to(row_max, (BLOCK, HEAD_DIM))
-        sum_ref[here(b), at] = jnp.broadcast_to(jnp.sum(weights, axis=1, keepdims=True), (BLOCK, HEAD_DIM))
+        max_ref[:, at] = jnp.broadcast_to(row_max, (rows, HEAD_DIM))
+        sum_ref[:, at] = jnp.broadcast_to(jnp.sum(weights, axis=1, keepdims=True), (rows, HEAD_DIM))
         return (weights.astype(jnp.bfloat16),)
 
-    def mix(b, h, weights):
-        at = slice(h * HEAD_DIM, (h + 1) * HEAD_DIM)
+    def mix(h, weights):
         v = kv_ref[:, cols + h * HEAD_DIM : cols + (h + 1) * HEAD_DIM]
-        mixed_ref[here(b), at] = jnp.dot(weights, v, preferred_element_type=jnp.float32)
-
-    pipelined([(b, h) for b in range(blocks) for h in range(cols // HEAD_DIM)], score, weigh, mix)
+        mixed_ref[:, h * HEAD_DIM : (h + 1) * HEAD_DIM] = jnp.dot(weights, v, preferred_element_type=jnp.float32)
+
+    pipelined([(h,) for h in range(cols // HEAD_DIM)], score, weigh, mix)
 
 
 def halo_kernel(*refs):
@@ -111,7 +109,7 @@
         add_halo(*others, two_ref, one_ref, out_ref)
 
 
-def add_halo(bias_ref, max_ref, sum_ref, mixed_ref, q_ref, left_ref, right_ref, out_ref):
+def add_halo(limit_ref, max_ref, sum_ref, mixed_ref, q_ref, left_ref, right_ref, out_ref):
     rows, cols = q_ref.shape
     blocks = rows // BLOCK
     factor = LOG2_E / HEAD_DIM**0.5
@@ -125,7 +123,8 @@
     def score(b, h):
         at = slice(h * HEAD_DIM, (h + 1) * HEAD_DIM)
         q = q_ref[here(b), at]
-        return jnp.concatenate([product(q, ref[part, at]) for ref, part in sides(b)], axis=1) + bias_ref[here(b), :]
+        products = [product(q, ref[part, at]) for ref, part in sides(b)]
+        return jnp.minimum(jnp.concatenate(products, axis=1), limit_ref[here(b), :])
 
     def weigh(b, h, scores):
         at = slice(h * HEAD_DIM, (h + 1) * HEAD_DIM)

time: 111 us -> 110 us (level)
  no operation moved by 1% of the time
where the time goes in v6:
time: 110 us
  blocking collectives  99.3 us (90%)
  Pallas kernels  5.92 us (5%)
  starting transfers between devices  2.68 us (2%)
  other arithmetic  1.38 us (1%)
    all_to_all x1, blocking collectives, body(): kv = lax.all_to_all(both, 'head', split_axis=1, concat_axis=0, tiled=True)  46.7 us
    all_to_all x1, blocking collectives, body(): q = lax.all_to_all(queries, 'head', split_axis=1, concat_axis=0, tiled=True)  26.6 us
    all_to_all x1, blocking collectives, body(): lax.all_to_all(mixed, 'head', split_axis=0, concat_axis=1, tiled=True)  26 us
    pallas_call x1, Pallas kernels, attend_halo(): pl.pallas_call(halo_kernel, out_shape=jax.ShapeDtypeStruct(q.shape, q.dty...  3.06 us
    pallas_call x1, Pallas kernels, attend_own(): pl.pallas_call(functools.partial(own_kernel, (span - 1) // 2, blocks_all)...  2.86 us
    ppermute x2, starting transfers between devices, body(): lax.ppermute(kv, ('seq', 'head'), [(i * groups + g, (i + step * (1 - 2 *...  2.68 us
  transfers between devices with their start and end apart: 2, of which 0 were waited for; matrix products, arithmetic and copies ran while one was open for 0% of the time, Pallas kernels for 3%

profile of v6, /device:TPU:1, one launch (start us, length us, event | category | flops | bytes accessed | tf_op | source)
XLA Modules:
  0.0 110.2 jit_solution(2837782364555061869)
XLA Ops:
  0.0 1.4 %pad_maximum_fusion = bf16[8,64,1280]{2,0,1:T(8,128)(2,1)S(1)} fusion(bf16[8,64,640]{2,0,1:T(8,128)(2,1)} %bitcast.22, bf16[8,64,640]{2,0,1:T(8,128)(2,1)} %bitcast.23), kind=kLoop, calls=%fused_computation | loop fusion | flops 2621440 | bytes 2621440 | tf_op jit(solution)/shard_map/concatenate | solution.py:185
  1.4 0.0 copy-start.2
  1.4 46.7 %all_to_all.54 = bf16[8,64,1280]{2,0,1:T(8,128)(2,1)S(1)} all-to-all(bf16[8,64,1280]{2,0,1:T(8,128)(2,1)S(1)} %pad_maximum_fusion), channel_id=1, replica_groups=mesh['seq'=4,'head'=64] {'head'}, dimensions={1} | all-to-all | bytes 2621440 | tf_op jit(solution)/shard_map/all_to_all | solution.py:188
  48.1 0.0 copy-start
  48.1 0.0 copy-start.1
  48.1 1.2 %collective-permute-start.1 = (bf16[512,1280]{1,0:T(8,128)(2,1)S(1)}, bf16[512,1280]{1,0:T(8,128)(2,1)S(1)}, u32[]{:S(2)}, u32[]{:S(2)}) collective-permute-start(bf16[512,1280]{1,0:T(8,128)(2,1)S(1)} %bitcast.16), channel_id=1, source_target_pairs={{0,192},{1,65},{2,194},{3,67},{4,196},{5,69},{6,198},{7,71},{8,200... | collective-permute-start | bytes 3932168 | tf_op jit(solution)/shard_map/ppermute | solution.py:190
  49.3 1.5 %collective-permute-start = (bf16[512,1280]{1,0:T(8,128)(2,1)S(1)}, bf16[512,1280]{1,0:T(8,128)(2,1)S(1)}, u32[]{:S(2)}, u32[]{:S(2)}) collective-permute-start(bf16[512,1280]{1,0:T(8,128)(2,1)S(1)} %bitcast.17), channel_id=1, source_target_pairs={{0,64},{1,193},{2,66},{3,195},{4,68},{5,197},{6,70},{7,199},{8,72}... | collective-permute-start | bytes 3932168 | tf_op jit(solution)/shard_map/ppermute | solution.py:190
  50.8 0.0 copy-done.2
  50.8 26.6 %all_to_all.55 = bf16[8,64,640]{2,0,1:T(8,128)(2,1)S(1)} all-to-all(bf16[8,64,640]{2,0,1:T(8,128)(2,1)S(1)} %bitcast.24), channel_id=1, replica_groups=mesh['seq'=4,'head'=64] {'head'}, dimensions={1} | all-to-all | bytes 1310720 | tf_op jit(solution)/shard_map/all_to_all | solution.py:201
  77.3 0.0 copy-done
  77.3 0.0 copy-done.1
  77.3 2.9 %shard_map.55 = (f32[512,640]{1,0:T(8,128)S(1)}, f32[512,640]{1,0:T(8,128)S(1)}, f32[512,640]{1,0:T(8,128)S(1)}, f32[512,640]{1,0:T(8,128)S(1)}) custom-call(s32[4]{0:T(128)S(1)} %copy-done.1, s32[9,1,16]{2,1,0:T(1,128)S(1)} %bitcast.20, bf16[512,640]{1,0:T(8,128)(2,1)S(1)} %bitcast.14, bf16[512,1280]{1,0:T(8,128)(2,1)S(1)} %bitcast.18), custom_call_target="tpu_custom_call" | custom-call | flops 1000 | bytes 1000 | tf_op jit(solution)/shard_map/pallas_call | solution.py:159
  80.2 0.0 collective-permute-done.1.refs_6_
  80.2 0.0 collective-permute-done.refs_5_
  80.2 3.1 %shard_map.56 = bf16[512,640]{1,0:T(8,128)(2,1)S(1)} custom-call(f32[512,640]{1,0:T(8,128)S(1)} %get-tuple-element.13.refs_0_, f32[512,640]{1,0:T(8,128)S(1)} %get-tuple-element.14.refs_1_, f32[512,640]{1,0:T(8,128)S(1)} %get-tuple-element.15.refs_2_, f32[512,640]{1,0:T(8,128)S(1)} %get-tuple-element.16.refs_3_, bf16[512,640]{1,0:T(8,128)(2,1)S(1)} %bitcast.15, ...), custom_call_target="tpu_custom_call" | custom-call | flops 900000000 | bytes 4000000 | tf_op jit(solution)/shard_map/pallas_call | solution.py:170
  83.3 26.0 %all_to_all.56 = bf16[64,8,640]{2,1,0:T(8,128)(2,1)S(1)} all-to-all(bf16[64,8,640]{2,1,0:T(8,128)(2,1)S(1)} %bitcast.19), channel_id=1, replica_groups=mesh['seq'=4,'head'=64] {'head'}, dimensions={0} | all-to-all | bytes 1310720 | tf_op jit(solution)/shard_map/all_to_all | solution.py:205
  109.3 0.8 copy.7
Async XLA Ops:
  1.4 49.4 %copy-start.2 = (bf16[8,40960]{1,0:T(8,128)(2,1)S(1)}, bf16[8,40960]{1,0:T(8,128)(2,1)}, u32[]{:S(2)}) copy-start(bf16[8,40960]{1,0:T(8,128)(2,1)} %param.5) | copy-start | bytes 1966084
  48.1 29.2 %copy-start = (s32[1,16,9]{1,0,2:T(1,128)S(1)}, s32[1,16,9]{1,0,2:T(1,128)}, u32[]{:S(2)}) copy-start(s32[1,16,9]{1,0,2:T(1,128)} %param.8) | copy-start | bytes 1732
  48.1 29.2 %copy-start.1 = (s32[4]{0:T(128)S(1)}, s32[4]{0:T(128)}, u32[]{:S(2)}) copy-start(s32[4]{0:T(128)} %lengths) | copy-start | bytes 52
  48.1 32.1 %collective-permute-start.1 = (bf16[512,1280]{1,0:T(8,128)(2,1)S(1)}, bf16[512,1280]{1,0:T(8,128)(2,1)S(1)}, u32[]{:S(2)}, u32[]{:S(2)}) collective-permute-start(bf16[512,1280]{1,0:T(8,128)(2,1)S(1)} %bitcast.16), channel_id=1, source_target_pairs={{0,192},{1,65},{2,194},{3,67},{4,196},{5,69},{6,198},{7,71},{8,200... | collective-permute-start | bytes 3932168 | tf_op jit(solution)/shard_map/ppermute | solution.py:190
  49.3 30.9 %collective-permute-start = (bf16[512,1280]{1,0:T(8,128)(2,1)S(1)}, bf16[512,1280]{1,0:T(8,128)(2,1)S(1)}, u32[]{:S(2)}, u32[]{:S(2)}) collective-permute-start(bf16[512,1280]{1,0:T(8,128)(2,1)S(1)} %bitcast.17), channel_id=1, source_target_pairs={{0,64},{1,193},{2,66},{3,195},{4,68},{5,197},{6,70},{7,199},{8,72}... | collective-permute-start | bytes 3932168 | tf_op jit(solution)/shard_map/ppermute | solution.py:190

commit v7 on v6

--- a/solution.py
+++ b/solution.py
@@ -46,11 +46,12 @@
 
 
 def pipelined(items, score, weigh, mix):
-    scored = {0: score(*items[0]), 1: score(*items[1])}
+    ahead = 3
+    scored = {i: score(*items[i]) for i in range(ahead)}
     weighed = {}
     for i in range(len(items) + 1):
-        if i + 2 < len(items):
-            scored[i + 2] = score(*items[i + 2])
+        if i + ahead < len(items):
+            scored[i + ahead] = score(*items[i + ahead])
         if i < len(items):
             weighed[i] = weigh(*items[i], scored.pop(i))
         if i > 0:

time: 110 us -> 111 us (level)
  no operation moved by 1% of the time
where the time goes in v7:
time: 111 us; the launch traced here: 110 us
  blocking collectives  99.3 us (89%)
  Pallas kernels  6.13 us (6%)
  starting transfers between devices  2.68 us (2%)
  other arithmetic  1.38 us (1%)
    all_to_all x1, blocking collectives, body(): kv = lax.all_to_all(both, 'head', split_axis=1, concat_axis=0, tiled=True)  46.7 us
    all_to_all x1, blocking collectives, body(): q = lax.all_to_all(queries, 'head', split_axis=1, concat_axis=0, tiled=True)  26.6 us
    all_to_all x1, blocking collectives, body(): lax.all_to_all(mixed, 'head', split_axis=0, concat_axis=1, tiled=True)  26 us
    pallas_call x1, Pallas kernels, attend_halo(): pl.pallas_call(halo_kernel, out_shape=jax.ShapeDtypeStruct(q.shape, q.dty...  3.25 us
    pallas_call x1, Pallas kernels, attend_own(): pl.pallas_call(functools.partial(own_kernel, (span - 1) // 2, blocks_all)...  2.88 us
    ppermute x2, starting transfers between devices, body(): lax.ppermute(kv, ('seq', 'head'), [(i * groups + g, (i + step * (1 - 2 *...  2.68 us
  transfers between devices with their start and end apart: 2, of which 0 were waited for; matrix products, arithmetic and copies ran while one was open for 0% of the time, Pallas kernels for 3%

profile of v7, /device:TPU:1, one launch (start us, length us, event | category | flops | bytes accessed | tf_op | source)
XLA Modules:
  0.0 110.4 jit_solution(11852228083442009116)
XLA Ops:
  0.0 1.4 %pad_maximum_fusion = bf16[8,64,1280]{2,0,1:T(8,128)(2,1)S(1)} fusion(bf16[8,64,640]{2,0,1:T(8,128)(2,1)} %bitcast.22, bf16[8,64,640]{2,0,1:T(8,128)(2,1)} %bitcast.23), kind=kLoop, calls=%fused_computation | loop fusion | flops 2621440 | bytes 2621440 | tf_op jit(solution)/shard_map/concatenate | solution.py:186
  1.4 0.0 copy-start.2
  1.4 46.7 %all_to_all.54 = bf16[8,64,1280]{2,0,1:T(8,128)(2,1)S(1)} all-to-all(bf16[8,64,1280]{2,0,1:T(8,128)(2,1)S(1)} %pad_maximum_fusion), channel_id=1, replica_groups=mesh['seq'=4,'head'=64] {'head'}, dimensions={1} | all-to-all | bytes 2621440 | tf_op jit(solution)/shard_map/all_to_all | solution.py:189
  48.1 0.0 copy-start
  48.1 0.0 copy-start.1
  48.1 1.2 %collective-permute-start.1 = (bf16[512,1280]{1,0:T(8,128)(2,1)S(1)}, bf16[512,1280]{1,0:T(8,128)(2,1)S(1)}, u32[]{:S(2)}, u32[]{:S(2)}) collective-permute-start(bf16[512,1280]{1,0:T(8,128)(2,1)S(1)} %bitcast.16), channel_id=1, source_target_pairs={{0,192},{1,65},{2,194},{3,67},{4,196},{5,69},{6,198},{7,71},{8,200... | collective-permute-start | bytes 3932168 | tf_op jit(solution)/shard_map/ppermute | solution.py:191
  49.3 1.5 %collective-permute-start = (bf16[512,1280]{1,0:T(8,128)(2,1)S(1)}, bf16[512,1280]{1,0:T(8,128)(2,1)S(1)}, u32[]{:S(2)}, u32[]{:S(2)}) collective-permute-start(bf16[512,1280]{1,0:T(8,128)(2,1)S(1)} %bitcast.17), channel_id=1, source_target_pairs={{0,64},{1,193},{2,66},{3,195},{4,68},{5,197},{6,70},{7,199},{8,72}... | collective-permute-start | bytes 3932168 | tf_op jit(solution)/shard_map/ppermute | solution.py:191
  50.8 0.0 copy-done.2
  50.8 26.6 %all_to_all.55 = bf16[8,64,640]{2,0,1:T(8,128)(2,1)S(1)} all-to-all(bf16[8,64,640]{2,0,1:T(8,128)(2,1)S(1)} %bitcast.24), channel_id=1, replica_groups=mesh['seq'=4,'head'=64] {'head'}, dimensions={1} | all-to-all | bytes 1310720 | tf_op jit(solution)/shard_map/all_to_all | solution.py:202
  77.3 0.0 copy-done
  77.3 0.0 copy-done.1
  77.3 2.9 %shard_map.55 = (f32[512,640]{1,0:T(8,128)S(1)}, f32[512,640]{1,0:T(8,128)S(1)}, f32[512,640]{1,0:T(8,128)S(1)}, f32[512,640]{1,0:T(8,128)S(1)}) custom-call(s32[4]{0:T(128)S(1)} %copy-done.1, s32[9,1,16]{2,1,0:T(1,128)S(1)} %bitcast.20, bf16[512,640]{1,0:T(8,128)(2,1)S(1)} %bitcast.14, bf16[512,1280]{1,0:T(8,128)(2,1)S(1)} %bitcast.18), custom_call_target="tpu_custom_call" | custom-call | flops 1000 | bytes 1000 | tf_op jit(solution)/shard_map/pallas_call | solution.py:160
  80.2 0.0 collective-permute-done.1.refs_6_
  80.2 0.0 collective-permute-done.refs_5_
  80.2 3.3 %shard_map.56 = bf16[512,640]{1,0:T(8,128)(2,1)S(1)} custom-call(f32[512,640]{1,0:T(8,128)S(1)} %get-tuple-element.13.refs_0_, f32[512,640]{1,0:T(8,128)S(1)} %get-tuple-element.14.refs_1_, f32[512,640]{1,0:T(8,128)S(1)} %get-tuple-element.15.refs_2_, f32[512,640]{1,0:T(8,128)S(1)} %get-tuple-element.16.refs_3_, bf16[512,640]{1,0:T(8,128)(2,1)S(1)} %bitcast.15, ...), custom_call_target="tpu_custom_call" | custom-call | flops 900000000 | bytes 4000000 | tf_op jit(solution)/shard_map/pallas_call | solution.py:171
  83.5 26.0 %all_to_all.56 = bf16[64,8,640]{2,1,0:T(8,128)(2,1)S(1)} all-to-all(bf16[64,8,640]{2,1,0:T(8,128)(2,1)S(1)} %bitcast.19), channel_id=1, replica_groups=mesh['seq'=4,'head'=64] {'head'}, dimensions={0} | all-to-all | bytes 1310720 | tf_op jit(solution)/shard_map/all_to_all | solution.py:206
  109.5 0.8 copy.7
Async XLA Ops:
  1.4 49.4 %copy-start.2 = (bf16[8,40960]{1,0:T(8,128)(2,1)S(1)}, bf16[8,40960]{1,0:T(8,128)(2,1)}, u32[]{:S(2)}) copy-start(bf16[8,40960]{1,0:T(8,128)(2,1)} %param.5) | copy-start | bytes 1966084
  48.1 29.2 %copy-start = (s32[1,16,9]{1,0,2:T(1,128)S(1)}, s32[1,16,9]{1,0,2:T(1,128)}, u32[]{:S(2)}) copy-start(s32[1,16,9]{1,0,2:T(1,128)} %param.8) | copy-start | bytes 1732
  48.1 29.2 %copy-start.1 = (s32[4]{0:T(128)S(1)}, s32[4]{0:T(128)}, u32[]{:S(2)}) copy-start(s32[4]{0:T(128)} %lengths) | copy-start | bytes 52
  48.1 32.1 %collective-permute-start.1 = (bf16[512,1280]{1,0:T(8,128)(2,1)S(1)}, bf16[512,1280]{1,0:T(8,128)(2,1)S(1)}, u32[]{:S(2)}, u32[]{:S(2)}) collective-permute-start(bf16[512,1280]{1,0:T(8,128)(2,1)S(1)} %bitcast.16), channel_id=1, source_target_pairs={{0,192},{1,65},{2,194},{3,67},{4,196},{5,69},{6,198},{7,71},{8,200... | collective-permute-start | bytes 3932168 | tf_op jit(solution)/shard_map/ppermute | solution.py:191
  49.3 30.9 %collective-permute-start = (bf16[512,1280]{1,0:T(8,128)(2,1)S(1)}, bf16[512,1280]{1,0:T(8,128)(2,1)S(1)}, u32[]{:S(2)}, u32[]{:S(2)}) collective-permute-start(bf16[512,1280]{1,0:T(8,128)(2,1)S(1)} %bitcast.17), channel_id=1, source_target_pairs={{0,64},{1,193},{2,66},{3,195},{4,68},{5,197},{6,70},{7,199},{8,72}... | collective-permute-start | bytes 3932168 | tf_op jit(solution)/shard_map/ppermute | solution.py:191
